TPU v7x, 32 devices: a whole 2x2x4 slice. The times are simulated.
32 devices in a mesh: chan: 8 (over z, y), grp: 4 (over x, core).
Axes of the slice: x: 2, y: 2, z: 4, core: 2. Of those that a mesh axis runs over, the one named last changes fastest.
Arguments:
- voltages: bfloat16 [512, 2, 139, 1024], P(('chan', 'grp')), may hold values from -6 to 6
- filter_taps: float32 [12, 512], replicated, may hold values from -1.75 to 1.75
- chan_index: int32 [96], replicated, may hold values from 0 to 511
- beam_weights: bfloat16 [96, 4096, 2, 512], P('chan', 'grp'), may hold values from -0.1875 to 0.1875
Outputs:
- beams: bfloat16 [96, 4096, 2, 2, 128], P('chan', 'grp')
Inputs may be any that keep to these rules, and one draw needn't show every extreme that they name: `chan_index`: filterbank channel numbers; a channel may be selected more than once.
All inputs are finite; a program needn't handle non-finite values.
Results may differ from a plain program's by a relative error of at most 0.0065.
Values may be sent and summed in bfloat16 or wider, within the bound.
No kernel may reach another device: no remote copies, remote signals or barrier semaphores. Data moves between devices by JAX's collectives and lax.ppermute only.
A program may use at most 192 MiB of HBM per device.

v0:
```python
import math

import jax
import jax.numpy as jnp
from jax import lax
from jax.sharding import PartitionSpec as P


def build_table(chan_index, fft_size):
    position = jnp.arange(fft_size, dtype=jnp.int32)
    phase = position[:, None] * chan_index[None, :] % fft_size
    angle = 2.0 * math.pi / fft_size * phase.astype(jnp.float32)
    factor = 1.0 / math.sqrt(fft_size)
    cosine = jnp.cos(angle) * factor
    sine = jnp.sin(angle) * factor
    upper = jnp.concatenate([cosine, -sine], axis=1)
    lower = jnp.concatenate([sine, cosine], axis=1)
    return jnp.concatenate([upper, lower], axis=0).astype(jnp.bfloat16)


def channelize(voltages, filter_taps, phase_table):
    tap_count = filter_taps.shape[0]
    spectra_count = voltages.shape[2] - tap_count + 1
    doubled = jnp.concatenate([filter_taps, filter_taps], axis=1)
    filtered = jnp.zeros(voltages.shape[:2] + (spectra_count, voltages.shape[3]), jnp.float32)
    for tap_delay in range(tap_count):
        window = voltages[:, :, tap_delay : tap_delay + spectra_count, :].astype(jnp.float32)
        filtered = filtered + window * doubled[tap_delay]
    filtered = filtered.astype(jnp.bfloat16)
    flat = filtered.reshape(-1, filtered.shape[3])
    result = jnp.dot(flat, phase_table, preferred_element_type=jnp.float32).astype(jnp.bfloat16)
    return result.reshape(voltages.shape[:2] + (spectra_count, 2, phase_table.shape[1] // 2))


def shards(voltages, filter_taps, chan_index, beam_weights):
    fft_size = filter_taps.shape[1]
    phase_table = build_table(chan_index, fft_size)
    spectra = channelize(voltages, filter_taps, phase_table)
    gathered = lax.all_gather(spectra, "grp", axis=0, tiled=True)
    turned = lax.all_to_all(gathered, "chan", split_axis=4, concat_axis=0, tiled=True)
    partial_value = jnp.einsum(
        "cbws,spmrc->cbwprm", beam_weights, turned, preferred_element_type=jnp.float32
    )
    real_part = partial_value[:, :, 0, :, 0] - partial_value[:, :, 1, :, 1]
    imag_part = partial_value[:, :, 0, :, 1] + partial_value[:, :, 1, :, 0]
    return jnp.stack([real_part, imag_part], axis=3).astype(jnp.bfloat16)


def solution(mesh):
    placed = (P(("chan", "grp"), None, None, None), P(), P(), P("chan", "grp", None, None))
    return jax.shard_map(
        shards,
        mesh=mesh,
        in_specs=placed,
        out_specs=P("chan", "grp", None, None, None),
        check_vma=False,
    )
```

profile of v0, /device:TPU:0, one launch (start us, length us, event | category | flops | bytes accessed | tf_op | source)
XLA Modules:
  0.0 468.3 jit_solution(4557955527916817182)
XLA Ops:
  6.5 0.0 copy-start
  6.5 0.0 copy-start.1
  6.5 0.0 all-gather.2.cloned.1.call-start
  6.5 102.7 %fusion.26 = (bf16[16,2,128,1024]{3,1,2,0:T(2,128)(2,1)}, bf16[16,2,128,1024]{3,1,2,0:T(2,128)(2,1)}, bf16[16,2,128,1024]{3,1,2,0:T(2,128)(2,1)}, bf16[16,2,128,...) fusion(bf16[16,2,139,1024]{3,1,2,0:T(2,128)(2,1)} %param.4), kind=kLoop, calls=%fused_computation.38 | loop fusion | bytes 201326592 | tf_op jit(solution)/shard_map/slice | solution.py:27
  109.2 0.0 copy-done
  109.3 0.0 copy-done.1
  109.3 1.1 negate_convert_fusion
  110.5 58.3 %add_convert_fusion = bf16[16,2,128,1024]{3,2,1,0:T(8,128)(2,1)} fusion(bf16[16,2,128,1024]{3,1,2,0:T(2,128)(2,1)} %get-tuple-element.16, bf16[16,2,128,1024]{3,1,2,0:T(2,128)(2,1)} %get-tuple-element.6, bf16[16,2,128,1024]{3,1,2,0:T(2,128)(2,1)} %get-tuple-element.7, bf16[16,2,128,1024]{3,1,2,0:T(2,128)(2,1)} %get-tuple-element.8, ...), kind=kLoop, calls=%fused_computation.3 | loop fusion | flops 150994944 | bytes 109101056 | tf_op jit(solution)/shard_map/convert_element_type | solution.py:29
  168.7 6.3 %convolution_convert_fusion = bf16[4096,192]{0,1:T(8,128)(2,1)S(1)} fusion(bf16[4096,1024]{1,0:T(8,128)(2,1)} %bitcast.46, bf16[512,96]{1,0:T(8,128)(2,1)S(1)} %get-tuple-element.31, bf16[512,96]{1,0:T(8,128)(2,1)S(1)} %get-tuple-element.30, bf16[512,96]{1,0:T(8,128)(2,1)S(1)} %get-tuple-element.29), kind=kOutput, calls=%fused_computation.14 | convolution fusion | flops 1612972032 | bytes 10256384 | tf_op jit(solution)/shard_map/dot_general | solution.py:31
  175.1 1.1 reshape.58
  176.2 1.6 copy.58
  177.8 0.0 all-gather.2.cloned.1.call-update
  177.8 50.1 %all-gather.2.cloned.1.call-done = bf16[64,2,128,2,96]{2,0,3,1,4:T(8,128)(2,1)} async-done(((bf16[16,2,128,2,96]{2,0,3,1,4:T(8,128)(2,1)}), bf16[64,2,128,2,96]{2,0,3,1,4:T(8,128)(2,1)}) %all-gather.2.cloned.1.call-update) | async-done | bytes 6291472 | tf_op jit(solution)/shard_map/all_gather | solution.py:39
  227.9 144.0 %all_to_all.18 = bf16[64,2,128,2,96]{2,0,3,1,4:T(8,128)(2,1)S(1)} all-to-all(bf16[64,2,128,2,96]{2,0,3,1,4:T(8,128)(2,1)} %all-gather.2.cloned.1.call-done), channel_id=1, replica_groups=mesh['chan'=8,'grp'=4] {'chan'}, dimensions={4} | all-to-all | bytes 12582912 | tf_op jit(solution)/shard_map/all_to_all | solution.py:40
  371.9 4.2 copy.60
  376.1 30.4 %fusion.2 = f32[12,1024,2,2,2,128]{1,5,2,4,3,0:T(8,128)} fusion(bf16[12,1024,2,512,1,1]{3,2,1,0,5,4:T(2,128)(2,1)} %bitcast.45, bf16[512,2,128,2,12,1]{2,0,4,3,1,5:T(8,128)(2,1)} %bitcast.44), kind=kOutput, calls=%fused_computation.2 | convolution fusion | flops 12884901888 | bytes 81788928 | tf_op jit(solution)/shard_map/cbws,spmrc->cbwprm/dot_general | solution.py:41
  406.5 9.3 %fusion.8 = bf16[12,1024,2,1,128]{1,4,2,0,3:T(8,128)(2,1)S(1)} fusion(f32[12,1024,2,2,2,128]{1,5,2,4,3,0:T(8,128)} %fusion.2), kind=kLoop, calls=%fused_computation.11 | loop fusion | flops 6291456 | bytes 31457280 | tf_op jit(solution)/shard_map/sub | solution.py:44
  415.8 9.2 %fusion.9 = bf16[12,1024,2,1,128]{1,4,2,0,3:T(8,128)(2,1)S(1)} fusion(f32[12,1024,2,2,2,128]{1,5,2,4,3,0:T(8,128)} %fusion.2), kind=kLoop, calls=%fused_computation.12 | loop fusion | flops 6291456 | bytes 31457280 | tf_op jit(solution)/shard_map/add | solution.py:45
  425.0 5.3 %pad_maximum_fusion = bf16[12,1024,2,2,128]{1,4,2,0,3:T(8,128)(2,1)} fusion(bf16[12,1024,2,1,128]{1,4,2,0,3:T(8,128)(2,1)S(1)} %fusion.9, bf16[12,1024,2,1,128]{1,4,2,0,3:T(8,128)(2,1)S(1)} %fusion.8), kind=kLoop, calls=%fused_computation.10 | loop fusion | flops 6291456 | bytes 25165824 | tf_op jit(solution)/shard_map/stack | solution.py:46
  430.3 31.1 %copy.65 = bf16[12,1024,2,2,128]{4,3,2,1,0:T(2,128)(2,1)} copy(bf16[12,1024,2,2,128]{1,4,2,0,3:T(8,128)(2,1)} %pad_maximum_fusion) | data formatting | bytes 25165824 | tf_op jit(solution)/shard_map/stack | solution.py:46
  (3 shorter events, 0.0 us)
Async XLA Ops:
  6.5 102.7 %copy-start = (f32[12,512]{1,0:T(8,128)S(1)}, f32[12,512]{1,0:T(8,128)}, u32[]{:S(2)}) copy-start(f32[12,512]{1,0:T(8,128)} %param.5) | copy-start | bytes 73732
  6.5 102.8 %copy-start.1 = (s32[96]{0:T(128)S(1)}, s32[96]{0:T(128)}, u32[]{:S(2)}) copy-start(s32[96]{0:T(128)} %param.6) | copy-start | bytes 1156
  6.5 221.4 %all-gather.2.cloned.1.call-start = ((), (), s32[]{:S(2)}) async-start(), calls=%async_computation.1 | async-start | bytes 7864320 | tf_op jit(solution)/shard_map/all_gather | solution.py:39
Sparse Core Ops, SparseCore 0:
  177.9 49.8 all-gather.1
where the time goes:
time: 469 us; the launch traced here: 468 us
  blocking collectives  144 us (31%)
  local copies, waits for them, and re-layouts  141 us (30%)
  other arithmetic  83.2 us (18%)
  waiting for transfers between devices  50.1 us (11%)
  matrix products  36.7 us (8%)
  between operations  13.5 us (3%)
    all_to_all x1, blocking collectives, shards(): lax.all_to_all(gathered, 'chan', split_axis=4, concat_axis=0, tiled=True)  144 us
    slice x1, local copies, waits for them, and re-layouts, channelize(): voltages[:, :, tap_delay:tap_delay + spectra_count, :].astype(jnp.float32)  103 us
    convert_element_type x1, other arithmetic, channelize(): filtered = filtered.astype(jnp.bfloat16)  58.3 us
    all_gather x1, waiting for transfers between devices, shards(): gathered = lax.all_gather(spectra, 'grp', axis=0, tiled=True)  50.1 us
    another operation x1, local copies, waits for them, and re-layouts, shards(): return jnp.stack([real_part, imag_part], axis=3).astype(jnp.bfloat16)  31.1 us
    dot_general x1, matrix products, shards(): jnp.einsum('cbws,spmrc->cbwprm', beam_weights, turned, preferred_element_...  30.4 us
  transfers between devices with their start and end apart: 1, of which 1 were waited for; matrix products, arithmetic and copies ran while one was open for 0% of the time, Pallas kernels for 0%

commit v1 on v0

v1 whole, which is shorter than its diff:
```python
import math, functools
import jax, jax.numpy as jnp
from jax import lax
from jax.experimental import pallas as pl
from jax.experimental.pallas import tpu as pltpu
from jax.sharding import PartitionSpec as P

def build_table_t(chan_index, fft_size):
    position = jnp.arange(fft_size, dtype=jnp.int32)
    phase = chan_index[:, None] * position[None, :] % fft_size
    angle = 2.0 * math.pi / fft_size * phase.astype(jnp.float32)
    factor = 1.0 / math.sqrt(fft_size)
    cosine = jnp.cos(angle) * factor
    sine = jnp.sin(angle) * factor
    first = jnp.concatenate([cosine, sine], axis=1)
    second = jnp.concatenate([-sine, cosine], axis=1)
    return jnp.concatenate([first, second], axis=0).astype(jnp.bfloat16)

def chan_kernel(stations, pols, spec, taps, group, v_ref, t_ref, f_ref, o_ref, fir, acc):
    s = pl.program_id(0)
    tiles = f_ref.shape[1] // 128
    lines = tiles * pols
    half = lines // 2
    nsel = f_ref.shape[0] // 2
    tap = [t_ref[pl.ds(t * half, half), :] for t in range(taps)]

    def step(i, _):
        m0 = i * group
        x = v_ref[0, pl.ds(pl.multiple_of(m0 * lines, lines), (group + taps - 1) * lines), :]
        x = x.astype(jnp.float32).reshape(group + taps - 1, 2, half, 128)
        for h in range(2):
            for g in range(group):
                total = x[g, h] * tap[0]
                for t in range(1, taps):
                    total = total + x[g + t, h] * tap[t]
                fir[pl.ds(pl.multiple_of((m0 + g) * lines, lines) + h * half, half), :] = total
        return 0

    lax.fori_loop(0, spec // group, step, 0)
    rows = []
    for p in range(pols):
        cols = [fir[pl.ds(nt * pols + p, spec, stride=lines), :].astype(jnp.bfloat16) for nt in range(tiles)]
        rows.append(jnp.concatenate(cols, axis=1))
    filtered = jnp.concatenate(rows, axis=0)
    out = lax.dot_general(f_ref[...], filtered, (((1,), (1,)), ((), ())), preferred_element_type=jnp.float32)
    for p in range(pols):
        for r in range(2):
            acc[pl.ds((p * 2 + r) * stations + s, nsel, stride=pols * 2 * stations), :] = (
                out[r * nsel:(r + 1) * nsel, p * spec:(p + 1) * spec])

    @pl.when(s == stations - 1)
    def _():
        o_ref[...] = acc[...].astype(jnp.bfloat16)

def channelize(voltages, filter_taps, table_t, group=8):
    stations, pols, blocks, width = voltages.shape
    taps, nfft = filter_taps.shape
    spec = blocks - taps + 1
    tiles = width // 128
    nsel = table_t.shape[0] // 2
    v = voltages.transpose(0, 2, 1, 3).reshape(stations, blocks, pols, tiles, 128)
    v = v.transpose(0, 1, 3, 2, 4).reshape(stations, blocks * tiles * pols, 128)
    half = tiles // 2 * pols
    t = jnp.repeat(filter_taps.reshape(taps * nfft // 128, 128), pols, axis=0)
    rows = nsel * pols * 2 * stations
    return pl.pallas_call(
        functools.partial(chan_kernel, stations, pols, spec, taps, group),
        grid=(stations,),
        out_shape=jax.ShapeDtypeStruct((rows, 128), jnp.bfloat16),
        in_specs=[
            pl.BlockSpec((1, blocks * tiles * pols, 128), lambda s: (s, 0, 0)),
            pl.BlockSpec((taps * half, 128), lambda s: (0, 0)),
            pl.BlockSpec(table_t.shape, lambda s: (0, 0)),
        ],
        out_specs=pl.BlockSpec((rows, 128), lambda s: (0, 0)),
        scratch_shapes=[pltpu.VMEM((spec * tiles * pols, 128), jnp.float32), pltpu.VMEM((rows, 128), jnp.float32)],
        compiler_params=pltpu.CompilerParams(vmem_limit_bytes=40 << 20),
        cost_estimate=pl.CostEstimate(flops=2 * stations * pols * spec * width * (taps*16 + 2 * nsel), bytes_accessed=voltages.size * 2, transcendentals=0),
        name="channelize",
    )(v, t, table_t)

def beam_kernel(sub, pr, w_ref, x_ref, o_ref, wide, rhs, outw):
    groups, chans, _, local, m = x_ref.shape
    local = local // pr
    stations = groups * chans * local
    st_n = stations // 128
    lines = st_n * 2
    for p in range(pr // 2):
        for c in range(chans):
            for g in range(groups):
                low = (c * groups + g) * local
                re = x_ref[g, c, 0, 2 * p * local:(2 * p + 1) * local, :]
                im = x_ref[g, c, 0, (2 * p + 1) * local:(2 * p + 2) * local, :]
                rhs[low:low + local, (2 * p) * m:(2 * p + 1) * m] = re
                rhs[low:low + local, (2 * p + 1) * m:(2 * p + 2) * m] = im
                rhs[stations + low:stations + low + local, (2 * p) * m:(2 * p + 1) * m] = -im
                rhs[stations + low:stations + low + local, (2 * p + 1) * m:(2 * p + 2) * m] = re
    beams = w_ref.shape[1] // lines
    tile = beams // sub
    right = rhs[...]
    for i in range(sub):
        wide[i] = w_ref[0, i * tile * lines:(i + 1) * tile * lines, :].astype(jnp.float32)
        left = jnp.concatenate(
            [wide[i, pl.ds(st * 2 + w, tile, stride=lines), :].astype(jnp.bfloat16) for w in range(2) for st in range(st_n)], axis=1)
        out = jnp.dot(left, right, preferred_element_type=jnp.float32)
        for q in range(pr):
            outw[i, pl.ds(q, tile, stride=pr), :] = out[:, q * m:(q + 1) * m]
        o_ref[0, i * tile * pr:(i + 1) * tile * pr, :] = outw[i].astype(jnp.bfloat16)

def beams_of(weights, x, pr, sub=4):
    chans, beams, parts, stations = weights.shape
    m = x.shape[4]
    st_n = stations // 128
    w = weights.reshape(chans, beams, 2, st_n, 128).transpose(0, 1, 3, 2, 4).reshape(chans, beams * st_n * 2, 128)
    tile = beams // sub
    out = pl.pallas_call(
        functools.partial(beam_kernel, sub, pr),
        grid=(chans,),
        out_shape=jax.ShapeDtypeStruct((chans, beams * pr, 128), jnp.bfloat16),
        in_specs=[
            pl.BlockSpec((1, beams * st_n * 2, 128), lambda j: (j, 0, 0)),
            pl.BlockSpec((x.shape[0], x.shape[1], 1, x.shape[3], m), lambda j: (0, 0, j, 0, 0)),
        ],
        out_specs=pl.BlockSpec((1, beams * pr, 128), lambda j: (j, 0, 0)),
        scratch_shapes=[pltpu.VMEM((sub, tile * st_n * 2, 128), jnp.float32), pltpu.VMEM((2 * stations, pr * m), jnp.bfloat16), pltpu.VMEM((sub, tile * pr, 128), jnp.float32)],
        compiler_params=pltpu.CompilerParams(vmem_limit_bytes=48 << 20),
        name="beams",
    )(w, x)
    return out.reshape(chans, beams, pr // 2, 2, m)


def shards(voltages, filter_taps, chan_index, beam_weights):
    stations, pols = voltages.shape[:2]
    chans = lax.axis_size("chan")
    table_t = build_table_t(chan_index, filter_taps.shape[1])
    spectra = channelize(voltages, filter_taps, table_t)
    mine = beam_weights.shape[0]
    spectra = spectra.reshape(chans, mine * pols * 2 * stations, 128)
    turned = lax.all_to_all(spectra, "chan", split_axis=0, concat_axis=0, tiled=True)
    gathered = lax.all_gather(turned, "grp", axis=0, tiled=False)
    x = gathered.reshape(gathered.shape[0], chans, mine, pols, 2, stations, 128)
    if stations % 16:
        x = x.transpose(2, 3, 4, 1, 0, 5, 6)
        x = x.reshape(1, 1, mine, -1, 128)
    else:
        x = x.reshape(x.shape[0], chans, mine, pols * 2 * stations, 128)
    return beams_of(beam_weights, x, pols * 2)


def solution(mesh):
    placed = (P(("chan", "grp"), None, None, None), P(), P(), P("chan", "grp", None, None))
    return jax.shard_map(
        shards,
        mesh=mesh,
        in_specs=placed,
        out_specs=P("chan", "grp", None, None, None),
        check_vma=False,
    )
```

time: 469 us -> 161 us (0.34)
  local copies, waits for them, and re-layouts: 141 us -> 4.36 us
  blocking collectives: 144 us -> 44.2 us
  other arithmetic: 83.2 us -> 1.56 us
  Pallas kernels: 0 us -> 50.8 us
  matrix products: 36.7 us -> 0 us
    slice x2 -> x0, local copies, waits for them, and re-layouts: 103 us -> none  [the longest x1 103 us: channelize(): voltages[:, :, tap_delay:tap_delay + spectra_count, :].astype(jnp.float32)]
    all_to_all x1, blocking collectives: 144 us -> 44.2 us  [shards(): lax.all_to_all(spectra, 'chan', split_axis=0, concat_axis=0, tiled=True)]
    convert_element_type x1 -> x0, other arithmetic: 58.3 us -> none  [channelize(): filtered = filtered.astype(jnp.bfloat16)]
    pallas_call x0 -> x2, Pallas kernels: none -> 50.8 us  [the longest x1 26.2 us: channelize(): pl.pallas_call(functools.partial(chan_kernel, stations, pols, spec, taps,...]
    dot_general x2 -> x0, matrix products: 36.7 us -> none  [the longest x1 30.4 us: shards(): jnp.einsum('cbws,spmrc->cbwprm', beam_weights, turned, preferred_element_...]
    another operation x1 -> x0, local copies, waits for them, and re-layouts: 31.1 us -> none  [shards(): return jnp.stack([real_part, imag_part], axis=3).astype(jnp.bfloat16)]
    sub x1 -> x0, other arithmetic: 9.27 us -> none  [shards(): real_part = partial_value[:, :, 0, :, 0] - partial_value[:, :, 1, :, 1]]
    add x1 -> x0, other arithmetic: 9.23 us -> none  [shards(): imag_part = partial_value[:, :, 0, :, 1] + partial_value[:, :, 1, :, 0]]
where the time goes in v1:
time: 161 us; the launch traced here: 160 us
  Pallas kernels  50.8 us (32%)
  waiting for transfers between devices  45.6 us (28%)
  blocking collectives  44.2 us (27%)
  between operations  13.4 us (8%)
  local copies, waits for them, and re-layouts  4.36 us (3%)
    all_gather x1, waiting for transfers between devices, shards(): gathered = lax.all_gather(turned, 'grp', axis=0, tiled=False)  45.5 us
    all_to_all x1, blocking collectives, shards(): lax.all_to_all(spectra, 'chan', split_axis=0, concat_axis=0, tiled=True)  44.2 us
    pallas_call x1, Pallas kernels, channelize(): pl.pallas_call(functools.partial(chan_kernel, stations, pols, spec, taps,...  26.2 us
    pallas_call x1, Pallas kernels, beams_of(): pl.pallas_call(functools.partial(beam_kernel, sub, pr), grid=(chans,), ou...  24.7 us
    unnamed x2, local copies, waits for them, and re-layouts  3.58 us
  transfers between devices with their start and end apart: 1, of which 1 were waited for; matrix products, arithmetic and copies ran while one was open for 0% of the time, Pallas kernels for 0%

profile of v1, /device:TPU:0, one launch (start us, length us, event | category | flops | bytes accessed | tf_op | source)
XLA Modules:
  0.0 159.9 jit_solution(1946954249922808528)
XLA Ops:
  6.5 0.0 all-gather.3.cloned.1.call-start
  6.5 0.8 reshape.29
  7.3 1.5 fusion.6
  8.9 0.0 copy-start
  8.9 3.6 %copy-done = bf16[16,2,139,1024]{3,1,2,0:T(2,128)(2,1)S(1)} copy-done((bf16[16,2,139,1024]{3,1,2,0:T(2,128)(2,1)S(1)}, bf16[16,2,139,1024]{3,1,2,0:T(2,128)(2,1)}, u32[]{:S(2)}) %copy-start) | copy-done | bytes 9109528
  12.5 26.2 %channelize.1 = bf16[6144,128]{1,0:T(8,128)(2,1)S(1)} custom-call(bf16[16,2224,128]{2,1,0:T(8,128)(2,1)S(1)} %bitcast.18, f32[96,128]{1,0:T(8,128)S(1)} %bitcast.17, bf16[192,1024]{1,0:T(8,128)(2,1)S(1)} %maximum_maximum_fusion.f_ref), custom_call_target="tpu_custom_call" | custom-call | flops 3221225472 | bytes 9109504 | tf_op jit(solution)/shard_map/channelize/pallas_call | solution.py:66
  38.7 44.2 %all_to_all.5 = bf16[8,768,128]{2,1,0:T(8,128)(2,1)} all-to-all(bf16[8,768,128]{2,1,0:T(8,128)(2,1)S(1)} %bitcast.16), channel_id=1, replica_groups=mesh['chan'=8,'grp'=4] {'chan'}, dimensions={0} | all-to-all | bytes 3145728 | tf_op jit(solution)/shard_map/all_to_all | solution.py:139
  82.9 0.0 all-gather.3.cloned.1.call-update
  82.9 45.5 %all-gather.3.cloned.1.call-done = bf16[32,768,128]{2,1,0:T(8,128)(2,1)} async-done(((bf16[8,768,128]{2,1,0:T(8,128)(2,1)}), bf16[32,768,128]{2,1,0:T(8,128)(2,1)}) %all-gather.3.cloned.1.call-update) | async-done | bytes 6291472 | tf_op jit(solution)/shard_map/all_gather | solution.py:140
  128.4 24.7 %beams.1 = bf16[12,4096,128]{2,1,0:T(8,128)(2,1)} custom-call(bf16[12,8192,128]{2,1,0:T(8,128)(2,1)} %bitcast.19, bf16[4,8,12,64,128]{4,3,2,1,0:T(8,128)(2,1)} %bitcast.20), custom_call_target="tpu_custom_call" | custom-call | tf_op jit(solution)/shard_map/beams/pallas_call | solution.py:116
  (2 shorter events, 0.0 us)
Async XLA Ops:
  6.5 121.9 %all-gather.3.cloned.1.call-start = ((), (), s32[]{:S(2)}) async-start(), calls=%async_computation.1 | async-start | bytes 7864320 | tf_op jit(solution)/shard_map/all_gather | solution.py:140
  8.9 3.6 %copy-start = (bf16[16,2,139,1024]{3,1,2,0:T(2,128)(2,1)S(1)}, bf16[16,2,139,1024]{3,1,2,0:T(2,128)(2,1)}, u32[]{:S(2)}) copy-start(bf16[16,2,139,1024]{3,1,2,0:T(2,128)(2,1)} %param.4) | copy-start | bytes 27328516
Sparse Core Ops, SparseCore 0:
  83.0 45.3 all-gather.2

commit v2 on v0

v2 whole, which is shorter than its diff:
```python
import functools
import math

import jax
import jax.numpy as jnp
from jax import lax
from jax.experimental import pallas as pl
from jax.experimental.pallas import tpu as pltpu
from jax.sharding import PartitionSpec as P

LANES = 128


def build_table(chan_index, fft_size):
    position = jnp.arange(fft_size, dtype=jnp.int32)
    phase = chan_index[:, None] * position[None, :] % fft_size
    angle = 2.0 * math.pi / fft_size * phase.astype(jnp.float32)
    factor = 1.0 / math.sqrt(fft_size)
    cosine = jnp.cos(angle) * factor
    sine = jnp.sin(angle) * factor
    first = jnp.concatenate([cosine, sine], axis=1)
    second = jnp.concatenate([-sine, cosine], axis=1)
    return jnp.concatenate([first, second], axis=0).astype(jnp.bfloat16)


def channelize_kernel(dims, v_ref, t_ref, f_ref, *rest):
    stations, pols, spec, taps, group, chans, counts = dims
    outs, (fir, acc) = rest[: len(counts)], rest[len(counts) :]
    s = pl.program_id(0)
    tiles = v_ref.shape[1] // (spec + taps - 1) // pols
    lines = tiles * pols
    half = lines // 2
    nsel = f_ref.shape[0] // 2
    tap = [t_ref[pl.ds(t * half, half), :] for t in range(taps)]

    def step(i, _):
        m0 = i * group
        start = pl.multiple_of(m0 * lines, lines)
        x = v_ref[0, pl.ds(start, (group + taps - 1) * lines), :]
        x = x.astype(jnp.float32).reshape(group + taps - 1, 2, half, LANES)
        for h in range(2):
            for g in range(group):
                total = x[g, h] * tap[0]
                for t in range(1, taps):
                    total = total + x[g + t, h] * tap[t]
                row = pl.multiple_of((m0 + g) * lines, lines)
                fir[pl.ds(row + h * half, half), :] = total
        return 0

    lax.fori_loop(0, spec // group, step, 0)
    rows = []
    for p in range(pols):
        cols = [fir[pl.ds(n * pols + p, spec, stride=lines), :].astype(jnp.bfloat16) for n in range(tiles)]
        rows.append(jnp.concatenate(cols, axis=1))
    filtered = jnp.concatenate(rows, axis=0)
    out = lax.dot_general(f_ref[...], filtered, (((1,), (1,)), ((), ())), preferred_element_type=jnp.float32)
    for p in range(pols):
        for r in range(2):
            acc[pl.ds((p * 2 + r) * stations + s, nsel, stride=pols * 2 * stations), :] = out[
                r * nsel : (r + 1) * nsel, p * spec : (p + 1) * spec
            ]

    @pl.when(s == stations - 1)
    def _():
        size = pols * 2 * stations
        mine = nsel // chans
        for c in range(chans):
            low = c * mine * size
            for out_ref, count in zip(outs, counts):
                out_ref[c] = acc[low : low + count * size, :].astype(jnp.bfloat16)
                low += count * size


def channelize(v, taps_rows, table, dims, first, vmem=62):
    stations, pols, spec, taps, group, chans, counts = dims
    nsel = table.shape[0] // 2
    size = pols * 2 * stations
    rows = v.shape[1]
    return pl.pallas_call(
        functools.partial(channelize_kernel, dims),
        grid=(stations,),
        out_shape=[pltpu.HBM((chans, count * size, LANES), jnp.bfloat16) for count in counts],
        in_specs=[
            pl.BlockSpec((1, rows, LANES), lambda s: (s + first, 0, 0)),
            pl.BlockSpec(taps_rows.shape, lambda s: (0, 0)),
            pl.BlockSpec(table.shape, lambda s: (0, 0)),
        ],
        out_specs=[pl.BlockSpec((chans, count * size, LANES), lambda s: (0, 0, 0)) for count in counts],
        scratch_shapes=[
            pltpu.VMEM((spec * rows // (spec + taps - 1), LANES), jnp.float32),
            pltpu.VMEM((nsel * size, LANES), jnp.float32),
        ],
        compiler_params=pltpu.CompilerParams(vmem_limit_bytes=vmem << 20),
        cost_estimate=pl.CostEstimate(
            flops=14 * 10**9 * stations // 16, bytes_accessed=stations * rows * 256, transcendentals=0
        ),
        name="channelize",
    )(v, taps_rows, table)


def beam_kernel(dims, me_ref, w_ref, *rest):
    sub, pr, halves, groups, aliased = dims
    xs = rest[: halves * groups]
    o_ref, wide, rhs, outw = rest[halves * groups + aliased :]
    chans, _, local, m = xs[0].shape
    local = local // pr
    stations = groups * chans * local * halves
    st_n = stations // LANES
    lines = st_n * 2
    me = me_ref[0]
    for d in range(groups):
        g = me ^ d
        for c in range(chans):
            low = pl.multiple_of((c * groups + g) * (local * halves), local * halves)
            for q in range(0, pr, 2):
                part = [
                    jnp.concatenate(
                        [xs[h * groups + d][c, 0, (q + r) * local : (q + r + 1) * local, :] for h in range(halves)], axis=0
                    )
                    for r in range(2)
                ]
                rhs[pl.ds(low, local * halves), q * m : (q + 1) * m] = part[0]
                rhs[pl.ds(low, local * halves), (q + 1) * m : (q + 2) * m] = part[1]
                rhs[pl.ds(stations + low, local * halves), q * m : (q + 1) * m] = -part[1]
                rhs[pl.ds(stations + low, local * halves), (q + 1) * m : (q + 2) * m] = part[0]
    beams = w_ref.shape[1] // lines
    tile = beams // sub
    right = rhs[...]
    for i in range(sub):
        wide[i] = w_ref[0, i * tile * lines : (i + 1) * tile * lines, :].astype(jnp.float32)
        left = jnp.concatenate(
            [
                wide[i, pl.ds(st * 2 + w, tile, stride=lines), :].astype(jnp.bfloat16)
                for w in range(2)
                for st in range(st_n)
            ],
            axis=1,
        )
        out = jnp.dot(left, right, preferred_element_type=jnp.float32)
        for q in range(pr):
            outw[i, pl.ds(q, tile, stride=pr), :] = out[:, q * m : (q + 1) * m]
        o_ref[0, i * tile * pr : (i + 1) * tile * pr, :] = outw[i].astype(jnp.bfloat16)


def form_beams(me, w, xs, lows, count, pr, halves, first, stations, so_far=None, sub=4):
    chans, _, local, m = xs[0].shape
    channels, rows = w.shape[:2]
    st_n = stations // LANES
    beams = rows // (2 * st_n)
    tile = beams // sub
    groups = len(xs) // halves
    aliased = so_far is not None
    operands = [me, w, *xs] + ([so_far] if aliased else [])
    return pl.pallas_call(
        functools.partial(beam_kernel, (sub, pr, halves, groups, int(aliased))),
        grid=(count,),
        out_shape=jax.ShapeDtypeStruct((channels, beams * pr, m), jnp.bfloat16),
        in_specs=[
            pl.BlockSpec(memory_space=pltpu.SMEM),
            pl.BlockSpec((1, rows, LANES), lambda j: (j + first, 0, 0)),
            *[
                pl.BlockSpec((chans, 1, local, m), functools.partial(lambda low, j: (0, j + low, 0, 0), low))
                for low in lows
            ],
            *([pl.BlockSpec(memory_space=pl.ANY)] if aliased else []),
        ],
        out_specs=pl.BlockSpec((1, beams * pr, m), lambda j: (j + first, 0, 0)),
        scratch_shapes=[
            pltpu.VMEM((sub, tile * st_n * 2, LANES), jnp.float32),
            pltpu.VMEM((2 * stations, pr * m), jnp.bfloat16),
            pltpu.VMEM((sub, tile * pr, m), jnp.float32),
        ],
        input_output_aliases={len(operands) - 1: 0} if aliased else {},
        compiler_params=pltpu.CompilerParams(vmem_limit_bytes=62 << 20),
        cost_estimate=pl.CostEstimate(
            flops=24 * 10**9 * count // 12, bytes_accessed=count * rows * 256, transcendentals=0
        ),
        name="beams",
    )(*operands)


def shards(voltages, filter_taps, chan_index, beam_weights):
    stations, pols, blocks, width = voltages.shape
    taps, fft_size = filter_taps.shape
    chans, groups = lax.axis_size("chan"), lax.axis_size("grp")
    mine, beams, parts, whole = beam_weights.shape
    spec = blocks - taps + 1
    tiles, pr, st_n = width // LANES, pols * 2, whole // LANES
    table = build_table(chan_index, fft_size)
    taps_rows = jnp.repeat(filter_taps.reshape(-1, LANES), pols, axis=0)
    v = voltages.transpose(0, 2, 1, 3).reshape(stations, blocks, pols, tiles, LANES)
    v = v.transpose(0, 1, 3, 2, 4).reshape(stations, blocks * tiles * pols, LANES)
    w = beam_weights.reshape(mine, beams, 2, st_n, LANES).transpose(0, 1, 3, 2, 4).reshape(mine, beams * st_n * 2, LANES)
    me = lax.axis_index("grp").astype(jnp.int32).reshape(1)

    if stations % 16:
        (spectra,) = channelize(v, taps_rows, table, (stations, pols, spec, taps, 8, chans, (mine,)), 0)
        turned = lax.all_to_all(spectra, "chan", split_axis=0, concat_axis=0, tiled=True)
        x = lax.all_gather(turned, "grp", axis=0, tiled=False)
        x = x.reshape(groups, chans, mine, pr, stations, spec).transpose(2, 3, 1, 0, 4, 5)
        x = x.reshape(1, mine, pr * whole, spec)
        out = form_beams(jnp.zeros_like(me), w, [x], [0], mine, pr, 1, 0, whole)
        return out.reshape(mine, beams, pols, 2, spec)

    local = stations // 2
    splits = ((mine,), COUNTS(mine))
    pieces = []
    for h, counts in enumerate(splits):
        spectra = channelize(v, taps_rows, table, (local, pols, spec, taps, GROUP, chans, counts), h * local)
        row, first = [], 0
        for part, count in zip(spectra, counts):
            turned = lax.all_to_all(part, "chan", split_axis=0, concat_axis=0, tiled=True)
            got = [turned] + [None] * (groups - 1)
            for d in range(2, groups, 2):
                got[d] = lax.ppermute(turned, "grp", [(g, g ^ d) for g in range(groups)])
            for d in range(0, groups, 2):
                got[d + 1] = lax.ppermute(got[d], "grp", [(g, g ^ 1) for g in range(groups)])
            row.append((first, count, [x.reshape(chans, count, pr * local, spec) for x in got]))
            first += count
        pieces.append(row)
    out = None
    for first, count, xs in pieces[1]:
        whole_xs = pieces[0][0][2]
        lows = [first] * groups + [0] * groups
        out = form_beams(me, w, whole_xs + xs, lows, count, pr, 2, first, whole, out)
    return out.reshape(mine, beams, pols, 2, spec)


GROUP = 16


def COUNTS(mine):
    return (mine // 2, mine - mine // 2)


def solution(mesh):
    placed = (P(("chan", "grp"), None, None, None), P(), P(), P("chan", "grp", None, None))
    return jax.shard_map(
        shards,
        mesh=mesh,
        in_specs=placed,
        out_specs=P("chan", "grp", None, None, None),
        check_vma=False,
    )
```

time: 469 us -> 114 us (0.24)
  blocking collectives: 144 us -> 0 us
  local copies, waits for them, and re-layouts: 141 us -> 2.27 us
  other arithmetic: 83.2 us -> 2.32 us
  Pallas kernels: 0 us -> 54.4 us
  matrix products: 36.7 us -> 0 us
  starting transfers between devices: 0.01 us -> 20 us
  waiting for transfers between devices: 50.1 us -> 33.2 us
  between operations: 13.5 us -> 0.07 us
    all_to_all x1 -> x0, blocking collectives: 144 us -> none  [shards(): lax.all_to_all(gathered, 'chan', split_axis=4, concat_axis=0, tiled=True)]
    slice x2 -> x0, local copies, waits for them, and re-layouts: 103 us -> none  [the longest x1 103 us: channelize(): voltages[:, :, tap_delay:tap_delay + spectra_count, :].astype(jnp.float32)]
    convert_element_type x1 -> x0, other arithmetic: 58.3 us -> none  [channelize(): filtered = filtered.astype(jnp.bfloat16)]
    pallas_call x0 -> x4, Pallas kernels: none -> 54.4 us  [the longest x2 27.8 us: channelize(): pl.pallas_call(functools.partial(channelize_kernel, dims), grid=(stations...]
    all_gather x1 -> x0, waiting for transfers between devices: 50.1 us -> none  [shards(): gathered = lax.all_gather(spectra, 'grp', axis=0, tiled=True)]
    dot_general x2 -> x0, matrix products: 36.7 us -> none  [the longest x1 30.4 us: shards(): jnp.einsum('cbws,spmrc->cbwprm', beam_weights, turned, preferred_element_...]
    another operation x1 -> x0, local copies, waits for them, and re-layouts: 31.1 us -> none  [shards(): return jnp.stack([real_part, imag_part], axis=3).astype(jnp.bfloat16)]
    all_to_all x0 -> x3, waiting for transfers between devices: none -> 22.9 us  [shards(): lax.all_to_all(part, 'chan', split_axis=0, concat_axis=0, tiled=True)]
  transfers between devices with their start and end apart: 1 -> 12, of which waited for: 1 -> 5; matrix products, arithmetic and copies ran while one was open for 0% -> 0% of each run, Pallas kernels for 0% -> 24%
where the time goes in v2:
time: 114 us; the launch traced here: 112 us
  Pallas kernels  54.4 us (48%)
  waiting for transfers between devices  33.2 us (29%)
  starting transfers between devices  20 us (18%)
  other arithmetic  2.32 us (2%)
  local copies, waits for them, and re-layouts  2.27 us (2%)
    pallas_call x2, Pallas kernels, channelize(): pl.pallas_call(functools.partial(channelize_kernel, dims), grid=(stations...  27.8 us
    pallas_call x2, Pallas kernels, form_beams(): pl.pallas_call(functools.partial(beam_kernel, (sub, pr, halves, groups, i...  26.6 us
    all_to_all x3, waiting for transfers between devices, shards(): lax.all_to_all(part, 'chan', split_axis=0, concat_axis=0, tiled=True)  22.9 us
    all_to_all x3, starting transfers between devices, shards(): lax.all_to_all(part, 'chan', split_axis=0, concat_axis=0, tiled=True)  14.5 us
    ppermute x3, waiting for transfers between devices, shards(): got[d] = lax.ppermute(turned, 'grp', [(g, g ^ d) for g in range(groups)])  10.3 us
    ppermute x3, starting transfers between devices, shards(): got[d] = lax.ppermute(turned, 'grp', [(g, g ^ d) for g in range(groups)])  4.49 us
  transfers between devices with their start and end apart: 12, of which 5 were waited for; matrix products, arithmetic and copies ran while one was open for 0% of the time, Pallas kernels for 24%

profile of v2, /device:TPU:0, one launch (start us, length us, event | category | flops | bytes accessed | tf_op | source)
XLA Modules:
  0.0 112.3 jit_solution(8170501530524697547)
XLA Ops:
  0.0 0.8 reshape.66
  0.8 1.5 %fusion.6 = (bf16[96,512]{1,0:T(8,128)(2,1)S(1)}, bf16[96,512]{1,0:T(8,128)(2,1)S(1)}, bf16[96,512]{1,0:T(8,128)(2,1)S(1)}) fusion(s32[96]{0:T(128)} %param.6), kind=kLoop, calls=%fused_computation.13 | loop fusion | flops 983040 | bytes 295296 | tf_op jit(solution)/shard_map/convert.5
  2.3 0.8 maximum_maximum_fusion.f_ref
  3.1 0.6 broadcast_in_dim.2
  3.7 13.9 %channelize.2 = bf16[8,384,128]{2,1,0:T(8,128)(2,1)} custom-call(bf16[16,2224,128]{2,1,0:T(8,128)(2,1)} %bitcast.39, f32[96,128]{1,0:T(8,128)} %bitcast.37, bf16[192,1024]{1,0:T(8,128)(2,1)} %maximum_maximum_fusion.f_ref), custom_call_target="tpu_custom_call" | custom-call | flops 7000000000 | bytes 4554752 | tf_op jit(solution)/shard_map/channelize/pallas_call | solution.py:79
  17.6 7.3 %all-to-all-start = ((bf16[8,384,128]{2,1,0:T(8,128)(2,1)}), bf16[8,384,128]{2,1,0:T(8,128)(2,1)S(1)}, u32[]{:S(2)}, u32[]{:S(2)}) async-start(bf16[8,384,128]{2,1,0:T(8,128)(2,1)} %channelize.2), calls=%async_computation | async-start | bytes 1572864 | tf_op jit(solution)/shard_map/all_to_all | solution.py:212
  24.9 13.9 %channelize.3 = (bf16[8,192,128]{2,1,0:T(8,128)(2,1)}, bf16[8,192,128]{2,1,0:T(8,128)(2,1)}) custom-call(bf16[16,2224,128]{2,1,0:T(8,128)(2,1)} %bitcast.40, f32[96,128]{1,0:T(8,128)} %bitcast.38, bf16[192,1024]{1,0:T(8,128)(2,1)} %maximum_maximum_fusion.f_ref), custom_call_target="tpu_custom_call" | custom-call | flops 7000000000 | bytes 4554752 | tf_op jit(solution)/shard_map/channelize/pallas_call | solution.py:79
  38.8 6.2 %all-to-all-done = bf16[8,384,128]{2,1,0:T(8,128)(2,1)S(1)} async-done(((bf16[8,384,128]{2,1,0:T(8,128)(2,1)}), bf16[8,384,128]{2,1,0:T(8,128)(2,1)S(1)}, u32[]{:S(2)}, u32[]{:S(2)}) %all-to-all-start) | async-done | bytes 786464 | tf_op jit(solution)/shard_map/all_to_all | solution.py:212
  45.0 3.6 %all-to-all-start.2 = ((bf16[8,192,128]{2,1,0:T(8,128)(2,1)}), bf16[8,192,128]{2,1,0:T(8,128)(2,1)S(1)}, u32[]{:S(2)}, u32[]{:S(2)}) async-start(bf16[8,192,128]{2,1,0:T(8,128)(2,1)} %get-tuple-element.8), calls=%async_computation.2 | async-start | bytes 786432 | tf_op jit(solution)/shard_map/all_to_all | solution.py:212
  48.6 1.5 %collective-permute-start.1 = (bf16[8,384,128]{2,1,0:T(8,128)(2,1)S(1)}, bf16[8,384,128]{2,1,0:T(8,128)(2,1)S(1)}, u32[]{:S(2)}, u32[]{:S(2)}) collective-permute-start(bf16[8,384,128]{2,1,0:T(8,128)(2,1)S(1)} %all-to-all-done), channel_id=1, source_target_pairs={{0,2},{1,3},{2,0},{3,1},{4,6},{5,7},{6,4},{7,5},{8,10},{9,11},{10,... | collective-permute-start | bytes 2359304 | tf_op jit(solution)/shard_map/ppermute | solution.py:215
  50.1 10.4 %all-to-all-done.2 = bf16[8,192,128]{2,1,0:T(8,128)(2,1)S(1)} async-done(((bf16[8,192,128]{2,1,0:T(8,128)(2,1)}), bf16[8,192,128]{2,1,0:T(8,128)(2,1)S(1)}, u32[]{:S(2)}, u32[]{:S(2)}) %all-to-all-start.2) | async-done | bytes 393248 | tf_op jit(solution)/shard_map/all_to_all | solution.py:212
  60.5 3.6 %all-to-all-start.1 = ((bf16[8,192,128]{2,1,0:T(8,128)(2,1)}), bf16[8,192,128]{2,1,0:T(8,128)(2,1)S(1)}, u32[]{:S(2)}, u32[]{:S(2)}) async-start(bf16[8,192,128]{2,1,0:T(8,128)(2,1)} %get-tuple-element.7), calls=%async_computation.1 | async-start | bytes 786432 | tf_op jit(solution)/shard_map/all_to_all | solution.py:212
  64.1 1.5 %collective-permute-start.7 = (bf16[8,192,128]{2,1,0:T(8,128)(2,1)S(1)}, bf16[8,192,128]{2,1,0:T(8,128)(2,1)}, u32[]{:S(2)}, u32[]{:S(2)}) collective-permute-start(bf16[8,192,128]{2,1,0:T(8,128)(2,1)S(1)} %all-to-all-done.2), channel_id=1, source_target_pairs={{0,2},{1,3},{2,0},{3,1},{4,6},{5,7},{6,4},{7,5},{8,10},{9,11},{10,... | collective-permute-start | bytes 1179656 | tf_op jit(solution)/shard_map/ppermute | solution.py:215
  65.6 0.0 collective-permute-start
  65.6 3.5 %collective-permute-done.1 = bf16[8,384,128]{2,1,0:T(8,128)(2,1)S(1)} collective-permute-done((bf16[8,384,128]{2,1,0:T(8,128)(2,1)S(1)}, bf16[8,384,128]{2,1,0:T(8,128)(2,1)S(1)}, u32[]{:S(2)}, u32[]{:S(2)}) %collective-permute-start.1) | collective-permute-done | bytes 786464 | tf_op jit(solution)/shard_map/ppermute | solution.py:215
  69.1 0.0 collective-permute-start.2
  69.1 0.5 collective-permute-start.6
  69.6 6.3 %all-to-all-done.1 = bf16[8,192,128]{2,1,0:T(8,128)(2,1)S(1)} async-done(((bf16[8,192,128]{2,1,0:T(8,128)(2,1)}), bf16[8,192,128]{2,1,0:T(8,128)(2,1)S(1)}, u32[]{:S(2)}, u32[]{:S(2)}) %all-to-all-start.1) | async-done | bytes 393248 | tf_op jit(solution)/shard_map/all_to_all | solution.py:212
  75.9 1.5 %collective-permute-start.4 = (bf16[8,192,128]{2,1,0:T(8,128)(2,1)S(1)}, bf16[8,192,128]{2,1,0:T(8,128)(2,1)}, u32[]{:S(2)}, u32[]{:S(2)}) collective-permute-start(bf16[8,192,128]{2,1,0:T(8,128)(2,1)S(1)} %all-to-all-done.1), channel_id=1, source_target_pairs={{0,2},{1,3},{2,0},{3,1},{4,6},{5,7},{6,4},{7,5},{8,10},{9,11},{10,... | collective-permute-start | bytes 1179656 | tf_op jit(solution)/shard_map/ppermute | solution.py:215
  77.4 0.0 collective-permute-done.7
  77.4 0.0 collective-permute-start.8
  77.4 0.0 collective-permute-done.6
  77.4 0.5 collective-permute-start.3
  77.9 6.9 %collective-permute-done.4 = bf16[8,192,128]{2,1,0:T(8,128)(2,1)} collective-permute-done((bf16[8,192,128]{2,1,0:T(8,128)(2,1)S(1)}, bf16[8,192,128]{2,1,0:T(8,128)(2,1)}, u32[]{:S(2)}, u32[]{:S(2)}) %collective-permute-start.4) | collective-permute-done | bytes 393248 | tf_op jit(solution)/shard_map/ppermute | solution.py:215
  84.8 0.0 collective-permute-start.5
  84.8 0.0 collective-permute-done.8
  84.8 0.0 collective-permute-done
  84.8 0.0 collective-permute-done.2
  84.8 0.9 copy-done.3
  85.7 13.3 %beams.2.rest_8_ = bf16[12,4096,128]{2,1,0:T(8,128)(2,1)} custom-call(s32[1]{0:T(128)} %bitcast.me_ref, bf16[12,8192,128]{2,1,0:T(8,128)(2,1)} %bitcast.27, bf16[8,12,32,128]{3,2,1,0:T(8,128)(2,1)} %bitcast.29, bf16[8,12,32,128]{3,2,1,0:T(8,128)(2,1)} %bitcast.34, bf16[8,12,32,128]{3,2,1,0:T(8,128)(2,1)} %bitcast.32, ...), custom_call_target="tpu_custom_call" | custom-call | flops 12000000000 | bytes 12582912 | tf_op jit(solution)/shard_map/beams/pallas_call | solution.py:154
  98.9 0.0 collective-permute-done.5
  98.9 13.3 %beams.3 = bf16[12,4096,128]{2,1,0:T(8,128)(2,1)} custom-call(s32[1]{0:T(128)} %bitcast.me_ref, bf16[12,8192,128]{2,1,0:T(8,128)(2,1)} %bitcast.28, bf16[8,12,32,128]{3,2,1,0:T(8,128)(2,1)} %bitcast.30, bf16[8,12,32,128]{3,2,1,0:T(8,128)(2,1)} %bitcast.35, bf16[8,12,32,128]{3,2,1,0:T(8,128)(2,1)} %bitcast.33, ...), custom_call_target="tpu_custom_call", output_to_operand_aliasing={{}: (10, {})} | custom-call | flops 12000000000 | bytes 12582912 | tf_op jit(solution)/shard_map/beams/pallas_call | solution.py:154
  (10 shorter events, 0.0 us)
Async XLA Ops:
  17.6 27.5 %all-to-all-start = ((bf16[8,384,128]{2,1,0:T(8,128)(2,1)}), bf16[8,384,128]{2,1,0:T(8,128)(2,1)S(1)}, u32[]{:S(2)}, u32[]{:S(2)}) async-start(bf16[8,384,128]{2,1,0:T(8,128)(2,1)} %channelize.2), calls=%async_computation | async-start | bytes 1572864 | tf_op jit(solution)/shard_map/all_to_all | solution.py:212
  45.0 40.6 %copy-start = (bf16[8,384,128]{2,1,0:T(8,128)(2,1)}, bf16[8,384,128]{2,1,0:T(8,128)(2,1)S(1)}, u32[]{:S(2)}) copy-start(bf16[8,384,128]{2,1,0:T(8,128)(2,1)S(1)} %all-to-all-done) | copy-start | bytes 2359300
  45.0 15.4 %all-to-all-start.2 = ((bf16[8,192,128]{2,1,0:T(8,128)(2,1)}), bf16[8,192,128]{2,1,0:T(8,128)(2,1)S(1)}, u32[]{:S(2)}, u32[]{:S(2)}) async-start(bf16[8,192,128]{2,1,0:T(8,128)(2,1)} %get-tuple-element.8), calls=%async_computation.2 | async-start | bytes 786432 | tf_op jit(solution)/shard_map/all_to_all | solution.py:212
  48.6 20.5 %collective-permute-start.1 = (bf16[8,384,128]{2,1,0:T(8,128)(2,1)S(1)}, bf16[8,384,128]{2,1,0:T(8,128)(2,1)S(1)}, u32[]{:S(2)}, u32[]{:S(2)}) collective-permute-start(bf16[8,384,128]{2,1,0:T(8,128)(2,1)S(1)} %all-to-all-done), channel_id=1, source_target_pairs={{0,2},{1,3},{2,0},{3,1},{4,6},{5,7},{6,4},{7,5},{8,10},{9,11},{10,... | collective-permute-start | bytes 2359304 | tf_op jit(solution)/shard_map/ppermute | solution.py:215
  60.5 25.2 %copy-start.4 = (bf16[8,192,128]{2,1,0:T(8,128)(2,1)}, bf16[8,192,128]{2,1,0:T(8,128)(2,1)S(1)}, u32[]{:S(2)}) copy-start(bf16[8,192,128]{2,1,0:T(8,128)(2,1)S(1)} %all-to-all-done.2) | copy-start | bytes 1179652
  60.5 15.4 %all-to-all-start.1 = ((bf16[8,192,128]{2,1,0:T(8,128)(2,1)}), bf16[8,192,128]{2,1,0:T(8,128)(2,1)S(1)}, u32[]{:S(2)}, u32[]{:S(2)}) async-start(bf16[8,192,128]{2,1,0:T(8,128)(2,1)} %get-tuple-element.7), calls=%async_computation.1 | async-start | bytes 786432 | tf_op jit(solution)/shard_map/all_to_all | solution.py:212
  64.1 13.3 %collective-permute-start.7 = (bf16[8,192,128]{2,1,0:T(8,128)(2,1)S(1)}, bf16[8,192,128]{2,1,0:T(8,128)(2,1)}, u32[]{:S(2)}, u32[]{:S(2)}) collective-permute-start(bf16[8,192,128]{2,1,0:T(8,128)(2,1)S(1)} %all-to-all-done.2), channel_id=1, source_target_pairs={{0,2},{1,3},{2,0},{3,1},{4,6},{5,7},{6,4},{7,5},{8,10},{9,11},{10,... | collective-permute-start | bytes 1179656 | tf_op jit(solution)/shard_map/ppermute | solution.py:215
  65.6 19.2 %collective-permute-start = (bf16[8,384,128]{2,1,0:T(8,128)(2,1)S(1)}, bf16[8,384,128]{2,1,0:T(8,128)(2,1)S(1)}, u32[]{:S(2)}, u32[]{:S(2)}) collective-permute-start(bf16[8,384,128]{2,1,0:T(8,128)(2,1)S(1)} %all-to-all-done), channel_id=1, source_target_pairs={{0,1},{1,0},{2,3},{3,2},{4,5},{5,4},{6,7},{7,6},{8,9},{9,8},{10,11... | collective-permute-start | bytes 2359304 | tf_op jit(solution)/shard_map/ppermute | solution.py:217
  69.1 16.6 %copy-start.2 = (bf16[8,384,128]{2,1,0:T(8,128)(2,1)}, bf16[8,384,128]{2,1,0:T(8,128)(2,1)S(1)}, u32[]{:S(2)}) copy-start(bf16[8,384,128]{2,1,0:T(8,128)(2,1)S(1)} %collective-permute-done.1) | copy-start | bytes 2359300
  69.1 15.7 %collective-permute-start.2 = (bf16[8,384,128]{2,1,0:T(8,128)(2,1)S(1)}, bf16[8,384,128]{2,1,0:T(8,128)(2,1)}, u32[]{:S(2)}, u32[]{:S(2)}) collective-permute-start(bf16[8,384,128]{2,1,0:T(8,128)(2,1)S(1)} %collective-permute-done.1), channel_id=1, source_target_pairs={{0,1},{1,0},{2,3},{3,2},{4,5},{5,4},{6,7},{7,6},{8,9},{9,8},{10,11... | collective-permute-start | bytes 2359304 | tf_op jit(solution)/shard_map/ppermute | solution.py:217
  69.1 8.3 %collective-permute-start.6 = (bf16[8,192,128]{2,1,0:T(8,128)(2,1)S(1)}, bf16[8,192,128]{2,1,0:T(8,128)(2,1)}, u32[]{:S(2)}, u32[]{:S(2)}) collective-permute-start(bf16[8,192,128]{2,1,0:T(8,128)(2,1)S(1)} %all-to-all-done.2), channel_id=1, source_target_pairs={{0,1},{1,0},{2,3},{3,2},{4,5},{5,4},{6,7},{7,6},{8,9},{9,8},{10,11... | collective-permute-start | bytes 1179656 | tf_op jit(solution)/shard_map/ppermute | solution.py:217
  75.9 23.0 %copy-start.1 = (bf16[8,192,128]{2,1,0:T(8,128)(2,1)}, bf16[8,192,128]{2,1,0:T(8,128)(2,1)S(1)}, u32[]{:S(2)}) copy-start(bf16[8,192,128]{2,1,0:T(8,128)(2,1)S(1)} %all-to-all-done.1) | copy-start | bytes 1179652
  75.9 8.9 %collective-permute-start.4 = (bf16[8,192,128]{2,1,0:T(8,128)(2,1)S(1)}, bf16[8,192,128]{2,1,0:T(8,128)(2,1)}, u32[]{:S(2)}, u32[]{:S(2)}) collective-permute-start(bf16[8,192,128]{2,1,0:T(8,128)(2,1)S(1)} %all-to-all-done.1), channel_id=1, source_target_pairs={{0,2},{1,3},{2,0},{3,1},{4,6},{5,7},{6,4},{7,5},{8,10},{9,11},{10,... | collective-permute-start | bytes 1179656 | tf_op jit(solution)/shard_map/ppermute | solution.py:215
  77.4 7.4 %collective-permute-start.8 = (bf16[8,192,128]{2,1,0:T(8,128)(2,1)}, bf16[8,192,128]{2,1,0:T(8,128)(2,1)}, u32[]{:S(2)}, u32[]{:S(2)}) collective-permute-start(bf16[8,192,128]{2,1,0:T(8,128)(2,1)} %collective-permute-done.7), channel_id=1, source_target_pairs={{0,1},{1,0},{2,3},{3,2},{4,5},{5,4},{6,7},{7,6},{8,9},{9,8},{10,11... | collective-permute-start | bytes 1179656 | tf_op jit(solution)/shard_map/ppermute | solution.py:217
  77.4 21.5 %collective-permute-start.3 = (bf16[8,192,128]{2,1,0:T(8,128)(2,1)S(1)}, bf16[8,192,128]{2,1,0:T(8,128)(2,1)}, u32[]{:S(2)}, u32[]{:S(2)}) collective-permute-start(bf16[8,192,128]{2,1,0:T(8,128)(2,1)S(1)} %all-to-all-done.1), channel_id=1, source_target_pairs={{0,1},{1,0},{2,3},{3,2},{4,5},{5,4},{6,7},{7,6},{8,9},{9,8},{10,11... | collective-permute-start | bytes 1179656 | tf_op jit(solution)/shard_map/ppermute | solution.py:217
  84.8 14.2 %collective-permute-start.5 = (bf16[8,192,128]{2,1,0:T(8,128)(2,1)}, bf16[8,192,128]{2,1,0:T(8,128)(2,1)}, u32[]{:S(2)}, u32[]{:S(2)}) collective-permute-start(bf16[8,192,128]{2,1,0:T(8,128)(2,1)} %collective-permute-done.4), channel_id=1, source_target_pairs={{0,1},{1,0},{2,3},{3,2},{4,5},{5,4},{6,7},{7,6},{8,9},{9,8},{10,11... | collective-permute-start | bytes 1179656 | tf_op jit(solution)/shard_map/ppermute | solution.py:217
  84.8 0.9 copy-start.3

commit v3 on v2

v3 whole, which is shorter than its diff:
```python
import functools
import math

import jax
import jax.numpy as jnp
from jax import lax
from jax.experimental import pallas as pl
from jax.experimental.pallas import tpu as pltpu
from jax.sharding import PartitionSpec as P

LANES = 128


def build_table(chan_index, fft_size):
    position = jnp.arange(fft_size, dtype=jnp.int32)
    phase = chan_index[:, None] * position[None, :] % fft_size
    angle = 2.0 * math.pi / fft_size * phase.astype(jnp.float32)
    factor = 1.0 / math.sqrt(fft_size)
    cosine = jnp.cos(angle) * factor
    sine = jnp.sin(angle) * factor
    first = jnp.concatenate([cosine, sine], axis=1)
    second = jnp.concatenate([-sine, cosine], axis=1)
    return jnp.concatenate([first, second], axis=0).astype(jnp.bfloat16)


def channelize_kernel(dims, v_ref, t_ref, f_ref, *rest):
    stations, pols, spec, taps, group, split, chans, counts = dims
    outs, (tap_rows, fir, acc) = rest[: len(counts)], rest[len(counts) :]
    s = pl.program_id(0)
    tiles = v_ref.shape[1] // (spec + taps - 1) // pols
    lines = tiles * pols
    half = lines // 2
    nsel = f_ref.shape[0] // 2

    @pl.when(s == 0)
    def _():
        for t in range(taps):
            for n in range(half // pols):
                row = t_ref[t : t + 1, n * LANES : (n + 1) * LANES]
                tap_rows[t * half + n * pols : t * half + (n + 1) * pols, :] = jnp.broadcast_to(row, (pols, LANES))

    def filter_part(slot, low, high):
        tap = [tap_rows[t * half : (t + 1) * half, :] for t in range(taps)]
        for m0 in range(low, high, group):
            x = v_ref[0, m0 * lines : (m0 + group + taps - 1) * lines, :]
            x = x.astype(jnp.float32).reshape(group + taps - 1, 2, half, LANES)
            for h in range(2):
                for g in range(group):
                    total = x[g, h] * tap[0]
                    for t in range(1, taps):
                        total = total + x[g + t, h] * tap[t]
                    row = (m0 + g) * (lines + 1) + h * half
                    fir[slot, row : row + half, :] = total

    def transform_part(slot, n0, n1):
        rows = []
        for p in range(pols):
            cols = [fir[slot, pl.ds(n * pols + p, spec, stride=lines + 1), :].astype(jnp.bfloat16) for n in range(n0, n1)]
            rows.append(jnp.concatenate(cols, axis=1))
        return lax.dot_general(
            f_ref[:, n0 * LANES : n1 * LANES],
            jnp.concatenate(rows, axis=0),
            (((1,), (1,)), ((), ())),
            preferred_element_type=jnp.float32,
        )

    def store(out, station):
        for p in range(pols):
            turned = out[:, p * spec : (p + 1) * spec]
            for r in range(2):
                acc[pl.ds((p * 2 + r) * stations + station, nsel, stride=pols * 2 * stations + 1), :] = turned[
                    r * nsel : (r + 1) * nsel, :
                ]

    def both(slot, old, do_filter, do_transform):
        out = None
        for i in range(split):
            if do_transform:
                part = transform_part(old, i * tiles // split, (i + 1) * tiles // split)
                out = part if out is None else out + part
            if do_filter:
                filter_part(slot, i * spec // split, (i + 1) * spec // split)
        if do_transform:
            store(out, s - 1)

    @pl.when(s == 0)
    def _():
        both(0, 1, True, False)

    for parity in range(2):
        @pl.when((s > 0) & (s < stations) & (lax.rem(s, 2) == parity))
        def _(parity=parity):
            both(parity, 1 - parity, True, True)

    @pl.when(s == stations)
    def _():
        both(0, (stations - 1) % 2, False, True)
        size = pols * 2 * stations
        mine = nsel // chans
        for c in range(chans):
            k = c * mine
            for out_ref, count in zip(outs, counts):
                for j in range(count):
                    rows = acc[k * (size + 1) : k * (size + 1) + size, :]
                    out_ref[c, j * size : (j + 1) * size, :] = rows.astype(jnp.bfloat16)
                    k += 1


def channelize(v, filter_taps, table, dims, first):
    stations, pols, spec, taps, group, split, chans, counts = dims
    nsel = table.shape[0] // 2
    size = pols * 2 * stations
    rows = v.shape[1]
    lines = rows // (spec + taps - 1)
    return pl.pallas_call(
        functools.partial(channelize_kernel, dims),
        grid=(stations + 1,),
        out_shape=[pltpu.HBM((chans, count * size, LANES), jnp.bfloat16) for count in counts],
        in_specs=[
            pl.BlockSpec((1, rows, LANES), lambda s: (jnp.minimum(s, stations - 1) + first, 0, 0)),
            pl.BlockSpec(filter_taps.shape, lambda s: (0, 0)),
            pl.BlockSpec(table.shape, lambda s: (0, 0)),
        ],
        out_specs=[pl.BlockSpec((chans, count * size, LANES), lambda s: (0, 0, 0)) for count in counts],
        scratch_shapes=[
            pltpu.VMEM((taps * lines // 2, LANES), jnp.float32),
            pltpu.VMEM((2, spec * (lines + 1), LANES), jnp.float32),
            pltpu.VMEM((nsel * (size + 1), LANES), jnp.float32),
        ],
        compiler_params=pltpu.CompilerParams(vmem_limit_bytes=62 << 20),
        cost_estimate=pl.CostEstimate(flops=14 * 10**9 * stations // 16, bytes_accessed=stations * rows * 256, transcendentals=0),
        name="channelize",
    )(v, filter_taps, table)


def beam_kernel(dims, me_ref, w_ref, *rest):
    sub, pr, halves, groups, aliased = dims
    for k in range(w_ref.shape[0]):
        one_channel(k, sub, pr, halves, groups, me_ref, w_ref, rest[: halves * groups], *rest[halves * groups + aliased :])


def one_channel(k, sub, pr, halves, groups, me_ref, w_ref, xs, o_ref, wide, rhs, outw):
    chans, _, local, m = xs[0].shape
    local = local // pr
    stations = groups * chans * local * halves
    st_n = stations // LANES
    lines = st_n * 2
    me = me_ref[0]
    for d in range(groups):
        g = me ^ d
        for c in range(chans):
            low = pl.multiple_of((c * groups + g) * (local * halves), local * halves)
            for q in range(0, pr, 2):
                part = [
                    jnp.concatenate(
                        [xs[h * groups + d][c, k, (q + r) * local : (q + r + 1) * local, :] for h in range(halves)], axis=0
                    )
                    for r in range(2)
                ]
                rhs[k % 2, pl.ds(low, local * halves), q * m : (q + 1) * m] = part[0]
                rhs[k % 2, pl.ds(low, local * halves), (q + 1) * m : (q + 2) * m] = part[1]
                rhs[k % 2, pl.ds(stations + low, local * halves), q * m : (q + 1) * m] = -part[1]
                rhs[k % 2, pl.ds(stations + low, local * halves), (q + 1) * m : (q + 2) * m] = part[0]
    beams = w_ref.shape[1] // lines
    tile = beams // sub
    right = rhs[k % 2]
    for i in range(sub):
        for b in range(0, tile, 2):
            low = (i * tile + b) * lines
            pair = w_ref[k, low : low + 2 * lines, :].astype(jnp.float32)
            wide[i, b * (lines + 1) : b * (lines + 1) + lines, :] = pair[:lines]
            wide[i, (b + 1) * (lines + 1) : (b + 1) * (lines + 1) + lines, :] = pair[lines:]
        left = jnp.concatenate(
            [
                wide[i, pl.ds(st * 2 + w, tile, stride=lines + 1), :].astype(jnp.bfloat16)
                for w in range(2)
                for st in range(st_n)
            ],
            axis=1,
        )
        out = jnp.dot(left, right, preferred_element_type=jnp.float32)
        for q in range(pr):
            outw[i, pl.ds(q, tile, stride=pr), :] = out[:, q * m : (q + 1) * m]
        o_ref[k, i * tile * pr : (i + 1) * tile * pr, :] = outw[i].astype(jnp.bfloat16)


def form_beams(me, w, xs, lows, count, pr, halves, first, stations, so_far=None, sub=4, each=1):
    chans, _, local, m = xs[0].shape
    channels, rows = w.shape[:2]
    st_n = stations // LANES
    beams = rows // (2 * st_n)
    tile = beams // sub
    groups = len(xs) // halves
    aliased = so_far is not None
    operands = [me, w, *xs] + ([so_far] if aliased else [])
    return pl.pallas_call(
        functools.partial(beam_kernel, (sub, pr, halves, groups, int(aliased))),
        grid=(count // each,),
        out_shape=jax.ShapeDtypeStruct((channels, beams * pr, m), jnp.bfloat16),
        in_specs=[
            pl.BlockSpec(memory_space=pltpu.SMEM),
            pl.BlockSpec((each, rows, LANES), lambda j: (j + first // each, 0, 0)),
            *[
                pl.BlockSpec((chans, each, local, m), functools.partial(lambda low, j: (0, j + low, 0, 0), low // each))
                for low in lows
            ],
            *([pl.BlockSpec(memory_space=pl.ANY)] if aliased else []),
        ],
        out_specs=pl.BlockSpec((each, beams * pr, m), lambda j: (j + first // each, 0, 0)),
        scratch_shapes=[
            pltpu.VMEM((sub, tile * (st_n * 2 + 1), LANES), jnp.float32),
            pltpu.VMEM((2, 2 * stations, pr * m), jnp.bfloat16),
            pltpu.VMEM((sub, tile * pr, m), jnp.float32),
        ],
        input_output_aliases={len(operands) - 1: 0} if aliased else {},
        compiler_params=pltpu.CompilerParams(vmem_limit_bytes=62 << 20),
        cost_estimate=pl.CostEstimate(
            flops=24 * 10**9 * count // 12, bytes_accessed=count * rows * 256, transcendentals=0
        ),
        name="beams",
    )(*operands)


def shards(voltages, filter_taps, chan_index, beam_weights):
    stations, pols, blocks, width = voltages.shape
    taps, fft_size = filter_taps.shape
    chans, groups = lax.axis_size("chan"), lax.axis_size("grp")
    mine, beams, parts, whole = beam_weights.shape
    spec = blocks - taps + 1
    tiles, pr, st_n = width // LANES, pols * 2, whole // LANES
    table = build_table(chan_index, fft_size)
    v = voltages.transpose(0, 2, 1, 3).reshape(stations, blocks, pols, tiles, LANES)
    v = v.transpose(0, 1, 3, 2, 4).reshape(stations, blocks * tiles * pols, LANES)
    w = beam_weights.reshape(mine, beams, 2, st_n, LANES).transpose(0, 1, 3, 2, 4).reshape(mine, beams * st_n * 2, LANES)
    me = lax.axis_index("grp").astype(jnp.int32).reshape(1)

    if stations % 16:
        (spectra,) = channelize(v, filter_taps, table, (stations, pols, spec, taps, 16, 4, chans, (mine,)), 0)
        turned = lax.all_to_all(spectra, "chan", split_axis=0, concat_axis=0, tiled=True)
        x = lax.all_gather(turned, "grp", axis=0, tiled=False)
        x = x.reshape(groups, chans, mine, pr, stations, spec).transpose(2, 3, 1, 0, 4, 5)
        x = x.reshape(1, mine, pr * whole, spec)
        out = form_beams(jnp.zeros_like(me), w, [x], [0], mine, pr, 1, 0, whole)
        return out.reshape(mine, beams, pols, 2, spec)

    local = stations // 2
    counts = COUNTS(mine)
    first_half, second_half = [
        channelize(v, filter_taps, table, (local, pols, spec, taps, 16, 4, chans, part), h * local)
        for h, part in enumerate(((mine,), counts))
    ]

    def turn(part):
        return lax.all_to_all(part, "chan", split_axis=0, concat_axis=0, tiled=True)

    def far(part):
        return {d: lax.ppermute(part, "grp", [(g, g ^ d) for g in range(groups)]) for d in range(2, groups, 2)}

    def near(part):
        return lax.ppermute(part, "grp", [(g, g ^ 1) for g in range(groups)])

    def pairs(own, others):
        return [x.reshape(chans, -1, pr * local, spec) for x in (own, near(own))] + others

    def spread(others):
        return [y.reshape(chans, -1, pr * local, spec) for x in others.values() for y in (x, near(x))]

    def beams_of(xs, i, out):
        first, size = sum(counts[:i]), counts[i]
        each = EACH if size % EACH == 0 and first % EACH == 0 else 1
        return form_beams(me, w, early + xs, [first] * groups + [0] * groups, size, pr, 2, first, whole, out, each=each)

    tie = lax.optimization_barrier
    turned = turn(first_half[0])
    turned, second_half = tie((turned, second_half))
    far_0 = far(turned)
    turned_a = turn(second_half[0])
    far_a = far(turned_a)
    turned_b = turn(second_half[1])
    far_0, far_a, turned_b = tie((far_0, far_a, turned_b))
    far_b = far(turned_b)
    early = pairs(turned, spread(far_0))
    out = beams_of(pairs(turned_a, spread(far_a)), 0, None)
    far_b, out = tie((far_b, out))
    out = beams_of(pairs(turned_b, spread(far_b)), 1, out)
    return out.reshape(mine, beams, pols, 2, spec)


EACH = 2


def COUNTS(mine):
    a = mine // 4 * 2
    return (a, mine - a)


def solution(mesh):
    placed = (P(("chan", "grp"), None, None, None), P(), P(), P("chan", "grp", None, None))
    return jax.shard_map(
        shards,
        mesh=mesh,
        in_specs=placed,
        out_specs=P("chan", "grp", None, None, None),
        check_vma=False,
    )
```

time: 114 us -> 105 us (0.921); the launches traced: 112 us -> 105 us
  Pallas kernels: 54.4 us -> 49.2 us
  local copies, waits for them, and re-layouts: 2.27 us -> 0.79 us
    ppermute x9, waiting for transfers between devices: 10.3 us -> 3.76 us  [the longest x6 3.32 us: near(): return lax.ppermute(part, 'grp', [(g, g ^ 1) for g in range(groups)])]
    all_to_all x3, waiting for transfers between devices: 22.9 us -> 28.9 us  [turn(): return lax.all_to_all(part, 'chan', split_axis=0, concat_axis=0, tiled=True)]
    pallas_call x2, Pallas kernels: 27.8 us -> 23.7 us  [channelize(): pl.pallas_call(functools.partial(channelize_kernel, dims), grid=(stations...]
  transfers between devices with their start and end apart: 12 -> 12, of which waited for: 5 -> 7; matrix products, arithmetic and copies ran while one was open for 0% -> 0% of each run, Pallas kernels for 24% -> 23%
where the time goes in v3:
time: 105 us
  Pallas kernels  49.2 us (47%)
  waiting for transfers between devices  32.6 us (31%)
  starting transfers between devices  20 us (19%)
  other arithmetic  2.32 us (2%)
    all_to_all x3, waiting for transfers between devices, turn(): return lax.all_to_all(part, 'chan', split_axis=0, concat_axis=0, tiled=True)  28.9 us
    pallas_call x2, Pallas kernels, form_beams(): pl.pallas_call(functools.partial(beam_kernel, (sub, pr, halves, groups, i...  25.5 us
    pallas_call x2, Pallas kernels, channelize(): pl.pallas_call(functools.partial(channelize_kernel, dims), grid=(stations...  23.7 us
    all_to_all x3, starting transfers between devices, turn(): return lax.all_to_all(part, 'chan', split_axis=0, concat_axis=0, tiled=True)  14.5 us
    ppermute x3, starting transfers between devices, far(): lax.ppermute(part, 'grp', [(g, g ^ d) for g in range(groups)])  4.54 us
    ppermute x6, waiting for transfers between devices, near(): return lax.ppermute(part, 'grp', [(g, g ^ 1) for g in range(groups)])  3.32 us
  transfers between devices with their start and end apart: 12, of which 7 were waited for; matrix products, arithmetic and copies ran while one was open for 0% of the time, Pallas kernels for 23%

profile of v3, /device:TPU:0, one launch (start us, length us, event | category | flops | bytes accessed | tf_op | source)
XLA Modules:
  0.0 105.0 jit_solution(6205665047012537730)
XLA Ops:
  0.0 1.5 %fusion.6 = (bf16[96,512]{1,0:T(8,128)(2,1)S(1)}, bf16[96,512]{1,0:T(8,128)(2,1)S(1)}, bf16[96,512]{1,0:T(8,128)(2,1)S(1)}) fusion(s32[96]{0:T(128)} %param.6), kind=kLoop, calls=%fused_computation.13 | loop fusion | flops 983040 | bytes 295296 | tf_op jit(solution)/shard_map/convert.5
  1.5 0.8 maximum_maximum_fusion.f_ref
  2.3 11.8 %channelize.2 = bf16[8,384,128]{2,1,0:T(8,128)(2,1)} custom-call(bf16[16,2224,128]{2,1,0:T(8,128)(2,1)} %bitcast.37, f32[12,512]{1,0:T(8,128)} %t_ref.3, bf16[192,1024]{1,0:T(8,128)(2,1)} %maximum_maximum_fusion.f_ref), custom_call_target="tpu_custom_call" | custom-call | flops 7000000000 | bytes 4554752 | tf_op jit(solution)/shard_map/channelize/pallas_call | solution.py:115
  14.1 7.3 %all-to-all-start = ((bf16[8,384,128]{2,1,0:T(8,128)(2,1)}), bf16[8,384,128]{2,1,0:T(8,128)(2,1)S(1)}, u32[]{:S(2)}, u32[]{:S(2)}) async-start(bf16[8,384,128]{2,1,0:T(8,128)(2,1)} %channelize.2), calls=%async_computation | async-start | bytes 1572864 | tf_op jit(solution)/shard_map/all_to_all | solution.py:254
  21.4 11.9 %channelize.3 = (bf16[8,192,128]{2,1,0:T(8,128)(2,1)}, bf16[8,192,128]{2,1,0:T(8,128)(2,1)}) custom-call(bf16[16,2224,128]{2,1,0:T(8,128)(2,1)} %bitcast.38, f32[12,512]{1,0:T(8,128)} %t_ref.3, bf16[192,1024]{1,0:T(8,128)(2,1)} %maximum_maximum_fusion.f_ref), custom_call_target="tpu_custom_call" | custom-call | flops 7000000000 | bytes 4554752 | tf_op jit(solution)/shard_map/channelize/pallas_call | solution.py:115
  33.3 8.3 %all-to-all-done = bf16[8,384,128]{2,1,0:T(8,128)(2,1)S(1)} async-done(((bf16[8,384,128]{2,1,0:T(8,128)(2,1)}), bf16[8,384,128]{2,1,0:T(8,128)(2,1)S(1)}, u32[]{:S(2)}, u32[]{:S(2)}) %all-to-all-start) | async-done | bytes 786464 | tf_op jit(solution)/shard_map/all_to_all | solution.py:254
  41.6 3.6 %all-to-all-start.1 = ((bf16[8,192,128]{2,1,0:T(8,128)(2,1)}), bf16[8,192,128]{2,1,0:T(8,128)(2,1)S(1)}, u32[]{:S(2)}, u32[]{:S(2)}) async-start(bf16[8,192,128]{2,1,0:T(8,128)(2,1)} %get-tuple-element.18), calls=%async_computation.1 | async-start | bytes 786432 | tf_op jit(solution)/shard_map/all_to_all | solution.py:254
  45.2 1.5 %collective-permute-start.1 = (bf16[8,384,128]{2,1,0:T(8,128)(2,1)S(1)}, bf16[8,384,128]{2,1,0:T(8,128)(2,1)S(1)}, u32[]{:S(2)}, u32[]{:S(2)}) collective-permute-start(bf16[8,384,128]{2,1,0:T(8,128)(2,1)S(1)} %all-to-all-done), channel_id=1, source_target_pairs={{0,2},{1,3},{2,0},{3,1},{4,6},{5,7},{6,4},{7,5},{8,10},{9,11},{10,... | collective-permute-start | bytes 2359304 | tf_op jit(solution)/shard_map/ppermute | solution.py:257
  46.7 10.4 %all-to-all-done.1 = bf16[8,192,128]{2,1,0:T(8,128)(2,1)S(1)} async-done(((bf16[8,192,128]{2,1,0:T(8,128)(2,1)}), bf16[8,192,128]{2,1,0:T(8,128)(2,1)S(1)}, u32[]{:S(2)}, u32[]{:S(2)}) %all-to-all-start.1) | async-done | bytes 393248 | tf_op jit(solution)/shard_map/all_to_all | solution.py:254
  57.0 3.6 %all-to-all-start.2 = ((bf16[8,192,128]{2,1,0:T(8,128)(2,1)}), bf16[8,192,128]{2,1,0:T(8,128)(2,1)S(1)}, u32[]{:S(2)}, u32[]{:S(2)}) async-start(bf16[8,192,128]{2,1,0:T(8,128)(2,1)} %get-tuple-element.19), calls=%async_computation.2 | async-start | bytes 786432 | tf_op jit(solution)/shard_map/all_to_all | solution.py:254
  60.7 1.6 %collective-permute-start.2 = (bf16[8,192,128]{2,1,0:T(8,128)(2,1)S(1)}, bf16[8,192,128]{2,1,0:T(8,128)(2,1)}, u32[]{:S(2)}, u32[]{:S(2)}) collective-permute-start(bf16[8,192,128]{2,1,0:T(8,128)(2,1)S(1)} %all-to-all-done.1), channel_id=1, source_target_pairs={{0,2},{1,3},{2,0},{3,1},{4,6},{5,7},{6,4},{7,5},{8,10},{9,11},{10,... | collective-permute-start | bytes 1179656 | tf_op jit(solution)/shard_map/ppermute | solution.py:257
  62.2 0.0 collective-permute-start
  62.2 10.2 %all-to-all-done.2 = bf16[8,192,128]{2,1,0:T(8,128)(2,1)S(1)} async-done(((bf16[8,192,128]{2,1,0:T(8,128)(2,1)}), bf16[8,192,128]{2,1,0:T(8,128)(2,1)S(1)}, u32[]{:S(2)}, u32[]{:S(2)}) %all-to-all-start.2) | async-done | bytes 393248 | tf_op jit(solution)/shard_map/all_to_all | solution.py:254
  72.4 0.0 collective-permute-done.1
  72.4 0.4 collective-permute-done.2
  72.9 0.0 collective-permute-start.3
  72.9 0.5 collective-permute-start.6
  73.4 0.0 collective-permute-start.7
  73.4 1.5 %collective-permute-start.5 = (bf16[8,192,128]{2,1,0:T(8,128)(2,1)S(1)}, bf16[8,192,128]{2,1,0:T(8,128)(2,1)}, u32[]{:S(2)}, u32[]{:S(2)}) collective-permute-start(bf16[8,192,128]{2,1,0:T(8,128)(2,1)S(1)} %all-to-all-done.2), channel_id=1, source_target_pairs={{0,2},{1,3},{2,0},{3,1},{4,6},{5,7},{6,4},{7,5},{8,10},{9,11},{10,... | collective-permute-start | bytes 1179656 | tf_op jit(solution)/shard_map/ppermute | solution.py:257
  74.9 0.0 collective-permute-done
  74.9 0.2 collective-permute-start.4
  75.1 1.3 %collective-permute-done.6 = bf16[8,192,128]{2,1,0:T(8,128)(2,1)} collective-permute-done((bf16[8,192,128]{2,1,0:T(8,128)(2,1)S(1)}, bf16[8,192,128]{2,1,0:T(8,128)(2,1)}, u32[]{:S(2)}, u32[]{:S(2)}) %collective-permute-start.6) | collective-permute-done | bytes 393248 | tf_op jit(solution)/shard_map/ppermute | solution.py:260
  76.4 0.2 collective-permute-done.7
  76.6 0.0 collective-permute-done.3
  76.6 0.0 copy-done.5
  76.7 12.8 %beams.2.rest_8_ = bf16[12,4096,128]{2,1,0:T(8,128)(2,1)} custom-call(s32[1]{0:T(128)} %bitcast.me_ref, bf16[12,8192,128]{2,1,0:T(8,128)(2,1)} %bitcast.26, bf16[8,12,32,128]{3,2,1,0:T(8,128)(2,1)} %bitcast.28, bf16[8,12,32,128]{3,2,1,0:T(8,128)(2,1)} %bitcast.33, bf16[8,12,32,128]{3,2,1,0:T(8,128)(2,1)} %bitcast.31, ...), custom_call_target="tpu_custom_call" | custom-call | flops 12000000000 | bytes 12582912 | tf_op jit(solution)/shard_map/beams/pallas_call | solution.py:196
  89.4 0.0 collective-permute-done.5
  89.4 0.2 collective-permute-start.8
  89.6 0.0 collective-permute-done.4
  89.6 1.8 %collective-permute-done.8 = bf16[8,192,128]{2,1,0:T(8,128)(2,1)S(1)} collective-permute-done((bf16[8,192,128]{2,1,0:T(8,128)(2,1)}, bf16[8,192,128]{2,1,0:T(8,128)(2,1)S(1)}, u32[]{:S(2)}, u32[]{:S(2)}) %collective-permute-start.8) | collective-permute-done | bytes 393248 | tf_op jit(solution)/shard_map/ppermute | solution.py:260
  91.4 0.8 copy-done.4
  92.2 12.8 %beams.3 = bf16[12,4096,128]{2,1,0:T(8,128)(2,1)} custom-call(s32[1]{0:T(128)} %bitcast.me_ref, bf16[12,8192,128]{2,1,0:T(8,128)(2,1)} %bitcast.27, bf16[8,12,32,128]{3,2,1,0:T(8,128)(2,1)} %bitcast.29, bf16[8,12,32,128]{3,2,1,0:T(8,128)(2,1)} %bitcast.34, bf16[8,12,32,128]{3,2,1,0:T(8,128)(2,1)} %bitcast.32, ...), custom_call_target="tpu_custom_call", output_to_operand_aliasing={{}: (10, {})} | custom-call | flops 12000000000 | bytes 12582912 | tf_op jit(solution)/shard_map/beams/pallas_call | solution.py:196
  (10 shorter events, 0.0 us)
Async XLA Ops:
  14.1 27.5 %all-to-all-start = ((bf16[8,384,128]{2,1,0:T(8,128)(2,1)}), bf16[8,384,128]{2,1,0:T(8,128)(2,1)S(1)}, u32[]{:S(2)}, u32[]{:S(2)}) async-start(bf16[8,384,128]{2,1,0:T(8,128)(2,1)} %channelize.2), calls=%async_computation | async-start | bytes 1572864 | tf_op jit(solution)/shard_map/all_to_all | solution.py:254
  41.6 35.0 %copy-start = (bf16[8,384,128]{2,1,0:T(8,128)(2,1)}, bf16[8,384,128]{2,1,0:T(8,128)(2,1)S(1)}, u32[]{:S(2)}) copy-start(bf16[8,384,128]{2,1,0:T(8,128)(2,1)S(1)} %all-to-all-done) | copy-start | bytes 2359300
  41.6 15.4 %all-to-all-start.1 = ((bf16[8,192,128]{2,1,0:T(8,128)(2,1)}), bf16[8,192,128]{2,1,0:T(8,128)(2,1)S(1)}, u32[]{:S(2)}, u32[]{:S(2)}) async-start(bf16[8,192,128]{2,1,0:T(8,128)(2,1)} %get-tuple-element.18), calls=%async_computation.1 | async-start | bytes 786432 | tf_op jit(solution)/shard_map/all_to_all | solution.py:254
  45.2 27.3 %collective-permute-start.1 = (bf16[8,384,128]{2,1,0:T(8,128)(2,1)S(1)}, bf16[8,384,128]{2,1,0:T(8,128)(2,1)S(1)}, u32[]{:S(2)}, u32[]{:S(2)}) collective-permute-start(bf16[8,384,128]{2,1,0:T(8,128)(2,1)S(1)} %all-to-all-done), channel_id=1, source_target_pairs={{0,2},{1,3},{2,0},{3,1},{4,6},{5,7},{6,4},{7,5},{8,10},{9,11},{10,... | collective-permute-start | bytes 2359304 | tf_op jit(solution)/shard_map/ppermute | solution.py:257
  57.0 19.6 %copy-start.5 = (bf16[8,192,128]{2,1,0:T(8,128)(2,1)}, bf16[8,192,128]{2,1,0:T(8,128)(2,1)S(1)}, u32[]{:S(2)}) copy-start(bf16[8,192,128]{2,1,0:T(8,128)(2,1)S(1)} %all-to-all-done.1) | copy-start | bytes 1179652
  57.0 15.4 %all-to-all-start.2 = ((bf16[8,192,128]{2,1,0:T(8,128)(2,1)}), bf16[8,192,128]{2,1,0:T(8,128)(2,1)S(1)}, u32[]{:S(2)}, u32[]{:S(2)}) async-start(bf16[8,192,128]{2,1,0:T(8,128)(2,1)} %get-tuple-element.19), calls=%async_computation.2 | async-start | bytes 786432 | tf_op jit(solution)/shard_map/all_to_all | solution.py:254
  60.7 12.2 %collective-permute-start.2 = (bf16[8,192,128]{2,1,0:T(8,128)(2,1)S(1)}, bf16[8,192,128]{2,1,0:T(8,128)(2,1)}, u32[]{:S(2)}, u32[]{:S(2)}) collective-permute-start(bf16[8,192,128]{2,1,0:T(8,128)(2,1)S(1)} %all-to-all-done.1), channel_id=1, source_target_pairs={{0,2},{1,3},{2,0},{3,1},{4,6},{5,7},{6,4},{7,5},{8,10},{9,11},{10,... | collective-permute-start | bytes 1179656 | tf_op jit(solution)/shard_map/ppermute | solution.py:257
  62.2 12.7 %collective-permute-start = (bf16[8,384,128]{2,1,0:T(8,128)(2,1)S(1)}, bf16[8,384,128]{2,1,0:T(8,128)(2,1)S(1)}, u32[]{:S(2)}, u32[]{:S(2)}) collective-permute-start(bf16[8,384,128]{2,1,0:T(8,128)(2,1)S(1)} %all-to-all-done), channel_id=1, source_target_pairs={{0,1},{1,0},{2,3},{3,2},{4,5},{5,4},{6,7},{7,6},{8,9},{9,8},{10,11... | collective-permute-start | bytes 2359304 | tf_op jit(solution)/shard_map/ppermute | solution.py:260
  72.4 17.0 %copy-start.1 = (bf16[8,192,128]{2,1,0:T(8,128)(2,1)}, bf16[8,192,128]{2,1,0:T(8,128)(2,1)S(1)}, u32[]{:S(2)}) copy-start(bf16[8,192,128]{2,1,0:T(8,128)(2,1)S(1)} %all-to-all-done.2) | copy-start | bytes 1179652
  72.4 4.2 %copy-start.2 = (bf16[8,384,128]{2,1,0:T(8,128)(2,1)}, bf16[8,384,128]{2,1,0:T(8,128)(2,1)S(1)}, u32[]{:S(2)}) copy-start(bf16[8,384,128]{2,1,0:T(8,128)(2,1)S(1)} %collective-permute-done.1) | copy-start | bytes 2359300
  72.9 3.8 %collective-permute-start.3 = (bf16[8,384,128]{2,1,0:T(8,128)(2,1)S(1)}, bf16[8,384,128]{2,1,0:T(8,128)(2,1)}, u32[]{:S(2)}, u32[]{:S(2)}) collective-permute-start(bf16[8,384,128]{2,1,0:T(8,128)(2,1)S(1)} %collective-permute-done.1), channel_id=1, source_target_pairs={{0,1},{1,0},{2,3},{3,2},{4,5},{5,4},{6,7},{7,6},{8,9},{9,8},{10,11... | collective-permute-start | bytes 2359304 | tf_op jit(solution)/shard_map/ppermute | solution.py:260
  72.9 3.5 %collective-permute-start.6 = (bf16[8,192,128]{2,1,0:T(8,128)(2,1)S(1)}, bf16[8,192,128]{2,1,0:T(8,128)(2,1)}, u32[]{:S(2)}, u32[]{:S(2)}) collective-permute-start(bf16[8,192,128]{2,1,0:T(8,128)(2,1)S(1)} %all-to-all-done.1), channel_id=1, source_target_pairs={{0,1},{1,0},{2,3},{3,2},{4,5},{5,4},{6,7},{7,6},{8,9},{9,8},{10,11... | collective-permute-start | bytes 1179656 | tf_op jit(solution)/shard_map/ppermute | solution.py:260
  73.4 3.2 %collective-permute-start.7 = (bf16[8,192,128]{2,1,0:T(8,128)(2,1)}, bf16[8,192,128]{2,1,0:T(8,128)(2,1)}, u32[]{:S(2)}, u32[]{:S(2)}) collective-permute-start(bf16[8,192,128]{2,1,0:T(8,128)(2,1)} %collective-permute-done.2), channel_id=1, source_target_pairs={{0,1},{1,0},{2,3},{3,2},{4,5},{5,4},{6,7},{7,6},{8,9},{9,8},{10,11... | collective-permute-start | bytes 1179656 | tf_op jit(solution)/shard_map/ppermute | solution.py:260
  73.4 16.0 %collective-permute-start.5 = (bf16[8,192,128]{2,1,0:T(8,128)(2,1)S(1)}, bf16[8,192,128]{2,1,0:T(8,128)(2,1)}, u32[]{:S(2)}, u32[]{:S(2)}) collective-permute-start(bf16[8,192,128]{2,1,0:T(8,128)(2,1)S(1)} %all-to-all-done.2), channel_id=1, source_target_pairs={{0,2},{1,3},{2,0},{3,1},{4,6},{5,7},{6,4},{7,5},{8,10},{9,11},{10,... | collective-permute-start | bytes 1179656 | tf_op jit(solution)/shard_map/ppermute | solution.py:257
  74.9 1.8 %copy-start.3 = (bf16[8,384,128]{2,1,0:T(8,128)(2,1)}, bf16[8,384,128]{2,1,0:T(8,128)(2,1)S(1)}, u32[]{:S(2)}) copy-start(bf16[8,384,128]{2,1,0:T(8,128)(2,1)S(1)} %collective-permute-done) | copy-start | bytes 2359300
  74.9 14.7 %collective-permute-start.4 = (bf16[8,192,128]{2,1,0:T(8,128)(2,1)S(1)}, bf16[8,192,128]{2,1,0:T(8,128)(2,1)}, u32[]{:S(2)}, u32[]{:S(2)}) collective-permute-start(bf16[8,192,128]{2,1,0:T(8,128)(2,1)S(1)} %all-to-all-done.2), channel_id=1, source_target_pairs={{0,1},{1,0},{2,3},{3,2},{4,5},{5,4},{6,7},{7,6},{8,9},{9,8},{10,11... | collective-permute-start | bytes 1179656 | tf_op jit(solution)/shard_map/ppermute | solution.py:260
  89.4 2.0 %collective-permute-start.8 = (bf16[8,192,128]{2,1,0:T(8,128)(2,1)}, bf16[8,192,128]{2,1,0:T(8,128)(2,1)S(1)}, u32[]{:S(2)}, u32[]{:S(2)}) collective-permute-start(bf16[8,192,128]{2,1,0:T(8,128)(2,1)} %collective-permute-done.5), channel_id=1, source_target_pairs={{0,1},{1,0},{2,3},{3,2},{4,5},{5,4},{6,7},{7,6},{8,9},{9,8},{10,11... | collective-permute-start | bytes 1179656 | tf_op jit(solution)/shard_map/ppermute | solution.py:260
  91.4 0.8 copy-start.4

commit v4 on v3

--- a/solution.py
+++ b/solution.py
@@ -11,21 +11,36 @@
 LANES = 128
 
 
-def build_table(chan_index, fft_size):
-    position = jnp.arange(fft_size, dtype=jnp.int32)
-    phase = chan_index[:, None] * position[None, :] % fft_size
-    angle = 2.0 * math.pi / fft_size * phase.astype(jnp.float32)
+def write_table(chan_ref, index_ref, f_ref):
+    nsel, fft_size = f_ref.shape[0] // 2, f_ref.shape[1] // 2
+    for k in range(nsel):
+        index_ref[k : k + 1, :] = jnp.full((1, LANES), chan_ref[k], jnp.int32)
+    index = index_ref[...]
+    lane = lax.broadcasted_iota(jnp.int32, (nsel, LANES), 1)
+
+    def parts(position):
+        phase = lax.rem(index * position, fft_size)
+        angle = 2.0 * math.pi / fft_size * phase.astype(jnp.float32)
+        return jnp.cos(angle), jnp.sin(angle)
+
     factor = 1.0 / math.sqrt(fft_size)
-    cosine = jnp.cos(angle) * factor
-    sine = jnp.sin(angle) * factor
-    first = jnp.concatenate([cosine, sine], axis=1)
-    second = jnp.concatenate([-sine, cosine], axis=1)
-    return jnp.concatenate([first, second], axis=0).astype(jnp.bfloat16)
-
-
-def channelize_kernel(dims, v_ref, t_ref, f_ref, *rest):
+    low_cos, low_sin = [x * factor for x in parts(lane)]
+    high_cos, high_sin = parts(lax.rem(lane * LANES, fft_size))
+    for h in range(fft_size // LANES):
+        c = jnp.broadcast_to(high_cos[:, h : h + 1], (nsel, LANES))
+        s = jnp.broadcast_to(high_sin[:, h : h + 1], (nsel, LANES))
+        cosine = (c * low_cos - s * low_sin).astype(jnp.bfloat16)
+        sine = (s * low_cos + c * low_sin).astype(jnp.bfloat16)
+        real, imag = h * LANES, fft_size + h * LANES
+        f_ref[:nsel, real : real + LANES] = cosine
+        f_ref[:nsel, imag : imag + LANES] = sine
+        f_ref[nsel:, real : real + LANES] = -sine
+        f_ref[nsel:, imag : imag + LANES] = cosine
+
+
+def channelize_kernel(dims, v_ref, t_ref, chan_ref, *rest):
     stations, pols, spec, taps, group, split, chans, counts = dims
-    outs, (tap_rows, fir, acc) = rest[: len(counts)], rest[len(counts) :]
+    outs, (index_ref, f_ref, tap_rows, fir, acc) = rest[: len(counts)], rest[len(counts) :]
     s = pl.program_id(0)
     tiles = v_ref.shape[1] // (spec + taps - 1) // pols
     lines = tiles * pols
@@ -34,6 +49,7 @@
 
     @pl.when(s == 0)
     def _():
+        write_table(chan_ref, index_ref, f_ref)
         for t in range(taps):
             for n in range(half // pols):
                 row = t_ref[t : t + 1, n * LANES : (n + 1) * LANES]
@@ -106,9 +122,9 @@
                     k += 1
 
 
-def channelize(v, filter_taps, table, dims, first):
+def channelize(v, filter_taps, chan_index, dims, first):
     stations, pols, spec, taps, group, split, chans, counts = dims
-    nsel = table.shape[0] // 2
+    nsel = chan_index.shape[0]
     size = pols * 2 * stations
     rows = v.shape[1]
     lines = rows // (spec + taps - 1)
@@ -119,18 +135,20 @@
         in_specs=[
             pl.BlockSpec((1, rows, LANES), lambda s: (jnp.minimum(s, stations - 1) + first, 0, 0)),
             pl.BlockSpec(filter_taps.shape, lambda s: (0, 0)),
-            pl.BlockSpec(table.shape, lambda s: (0, 0)),
+            pl.BlockSpec(memory_space=pltpu.SMEM),
         ],
         out_specs=[pl.BlockSpec((chans, count * size, LANES), lambda s: (0, 0, 0)) for count in counts],
         scratch_shapes=[
+            pltpu.VMEM((nsel, LANES), jnp.int32),
+            pltpu.VMEM((2 * nsel, 2 * filter_taps.shape[1]), jnp.bfloat16),
             pltpu.VMEM((taps * lines // 2, LANES), jnp.float32),
-            pltpu.VMEM((2, spec * (lines + 1), LANES), jnp.float32),
-            pltpu.VMEM((nsel * (size + 1), LANES), jnp.float32),
+            pltpu.VMEM((2, (spec + 2) * (lines + 1), LANES), jnp.float32),
+            pltpu.VMEM(((nsel + 2) * (size + 1), LANES), jnp.float32),
         ],
         compiler_params=pltpu.CompilerParams(vmem_limit_bytes=62 << 20),
         cost_estimate=pl.CostEstimate(flops=14 * 10**9 * stations // 16, bytes_accessed=stations * rows * 256, transcendentals=0),
         name="channelize",
-    )(v, filter_taps, table)
+    )(v, filter_taps, chan_index)
 
 
 def beam_kernel(dims, me_ref, w_ref, *rest):
@@ -181,7 +199,7 @@
         out = jnp.dot(left, right, preferred_element_type=jnp.float32)
         for q in range(pr):
             outw[i, pl.ds(q, tile, stride=pr), :] = out[:, q * m : (q + 1) * m]
-        o_ref[k, i * tile * pr : (i + 1) * tile * pr, :] = outw[i].astype(jnp.bfloat16)
+        o_ref[k, i * tile * pr : (i + 1) * tile * pr, :] = outw[i, : tile * pr, :].astype(jnp.bfloat16)
 
 
 def form_beams(me, w, xs, lows, count, pr, halves, first, stations, so_far=None, sub=4, each=1):
@@ -208,9 +226,9 @@
         ],
         out_specs=pl.BlockSpec((each, beams * pr, m), lambda j: (j + first // each, 0, 0)),
         scratch_shapes=[
-            pltpu.VMEM((sub, tile * (st_n * 2 + 1), LANES), jnp.float32),
+            pltpu.VMEM((sub, (tile + 8) * (st_n * 2 + 1), LANES), jnp.float32),
             pltpu.VMEM((2, 2 * stations, pr * m), jnp.bfloat16),
-            pltpu.VMEM((sub, tile * pr, m), jnp.float32),
+            pltpu.VMEM((sub, (tile + 8) * pr, m), jnp.float32),
         ],
         input_output_aliases={len(operands) - 1: 0} if aliased else {},
         compiler_params=pltpu.CompilerParams(vmem_limit_bytes=62 << 20),
@@ -228,14 +246,13 @@
     mine, beams, parts, whole = beam_weights.shape
     spec = blocks - taps + 1
     tiles, pr, st_n = width // LANES, pols * 2, whole // LANES
-    table = build_table(chan_index, fft_size)
     v = voltages.transpose(0, 2, 1, 3).reshape(stations, blocks, pols, tiles, LANES)
     v = v.transpose(0, 1, 3, 2, 4).reshape(stations, blocks * tiles * pols, LANES)
     w = beam_weights.reshape(mine, beams, 2, st_n, LANES).transpose(0, 1, 3, 2, 4).reshape(mine, beams * st_n * 2, LANES)
     me = lax.axis_index("grp").astype(jnp.int32).reshape(1)
 
     if stations % 16:
-        (spectra,) = channelize(v, filter_taps, table, (stations, pols, spec, taps, 16, 4, chans, (mine,)), 0)
+        (spectra,) = channelize(v, filter_taps, chan_index, (stations, pols, spec, taps, 16, 4, chans, (mine,)), 0)
         turned = lax.all_to_all(spectra, "chan", split_axis=0, concat_axis=0, tiled=True)
         x = lax.all_gather(turned, "grp", axis=0, tiled=False)
         x = x.reshape(groups, chans, mine, pr, stations, spec).transpose(2, 3, 1, 0, 4, 5)
@@ -246,7 +263,7 @@
     local = stations // 2
     counts = COUNTS(mine)
     first_half, second_half = [
-        channelize(v, filter_taps, table, (local, pols, spec, taps, 16, 4, chans, part), h * local)
+        channelize(v, filter_taps, chan_index, (local, pols, spec, taps, 16, 4, chans, part), h * local)
         for h, part in enumerate(((mine,), counts))
     ]
 
@@ -277,7 +294,7 @@
     turned_a = turn(second_half[0])
     far_a = far(turned_a)
     turned_b = turn(second_half[1])
-    far_0, far_a, turned_b = tie((far_0, far_a, turned_b))
+    far_a, turned_b = tie((far_a, turned_b))
     far_b = far(turned_b)
     early = pairs(turned, spread(far_0))
     out = beams_of(pairs(turned_a, spread(far_a)), 0, None)

time: 105 us -> 102 us (0.971)
  other arithmetic: 2.32 us -> 0 us
  waiting for transfers between devices: 32.6 us -> 30.4 us
    all_to_all x3, waiting for transfers between devices: 28.9 us -> 24.5 us  [turn(): return lax.all_to_all(part, 'chan', split_axis=0, concat_axis=0, tiled=True)]
    ppermute x3, waiting for transfers between devices: 0.44 us -> 3.82 us  [far(): lax.ppermute(part, 'grp', [(g, g ^ d) for g in range(groups)])]
    another operation x1 -> x0, other arithmetic: 1.53 us -> none
    ppermute x6, waiting for transfers between devices: 3.32 us -> 2.04 us  [near(): return lax.ppermute(part, 'grp', [(g, g ^ 1) for g in range(groups)])]
  transfers between devices with their start and end apart: 12 -> 12, of which waited for: 7 -> 7; matrix products, arithmetic and copies ran while one was open for 0% -> 0% of each run, Pallas kernels for 23% -> 25%
where the time goes in v4:
time: 102 us
  Pallas kernels  50 us (49%)
  waiting for transfers between devices  30.4 us (30%)
  starting transfers between devices  20.1 us (20%)
  local copies, waits for them, and re-layouts  1.09 us (1%)
    pallas_call x2, Pallas kernels, form_beams(): pl.pallas_call(functools.partial(beam_kernel, (sub, pr, halves, groups, i...  25.5 us
    pallas_call x2, Pallas kernels, channelize(): pl.pallas_call(functools.partial(channelize_kernel, dims), grid=(stations...  24.5 us
    all_to_all x3, waiting for transfers between devices, turn(): return lax.all_to_all(part, 'chan', split_axis=0, concat_axis=0, tiled=True)  24.5 us
    all_to_all x3, starting transfers between devices, turn(): return lax.all_to_all(part, 'chan', split_axis=0, concat_axis=0, tiled=True)  14.5 us
    ppermute x3, starting transfers between devices, far(): lax.ppermute(part, 'grp', [(g, g ^ d) for g in range(groups)])  4.57 us
    ppermute x3, waiting for transfers between devices, far(): lax.ppermute(part, 'grp', [(g, g ^ d) for g in range(groups)])  3.82 us
    ppermute x6, waiting for transfers between devices, near(): return lax.ppermute(part, 'grp', [(g, g ^ 1) for g in range(groups)])  2.04 us
  transfers between devices with their start and end apart: 12, of which 7 were waited for; matrix products, arithmetic and copies ran while one was open for 0% of the time, Pallas kernels for 25%

profile of v4, /device:TPU:0, one launch (start us, length us, event | category | flops | bytes accessed | tf_op | source)
XLA Modules:
  0.0 101.6 jit_solution(2624262386286706923)
XLA Ops:
  0.0 12.2 %channelize.2 = bf16[8,384,128]{2,1,0:T(8,128)(2,1)} custom-call(bf16[16,2224,128]{2,1,0:T(8,128)(2,1)} %bitcast.37, f32[12,512]{1,0:T(8,128)} %t_ref.3, s32[96]{0:T(128)} %chan_ref.3), custom_call_target="tpu_custom_call" | custom-call | flops 7000000000 | bytes 4554752 | tf_op jit(solution)/shard_map/channelize/pallas_call | solution.py:131
  12.2 7.3 %all-to-all-start = ((bf16[8,384,128]{2,1,0:T(8,128)(2,1)}), bf16[8,384,128]{2,1,0:T(8,128)(2,1)S(1)}, u32[]{:S(2)}, u32[]{:S(2)}) async-start(bf16[8,384,128]{2,1,0:T(8,128)(2,1)} %channelize.2), calls=%async_computation | async-start | bytes 1572864 | tf_op jit(solution)/shard_map/all_to_all | solution.py:271
  19.5 12.3 %channelize.3 = (bf16[8,192,128]{2,1,0:T(8,128)(2,1)}, bf16[8,192,128]{2,1,0:T(8,128)(2,1)}) custom-call(bf16[16,2224,128]{2,1,0:T(8,128)(2,1)} %bitcast.38, f32[12,512]{1,0:T(8,128)} %t_ref.3, s32[96]{0:T(128)} %chan_ref.3), custom_call_target="tpu_custom_call" | custom-call | flops 7000000000 | bytes 4554752 | tf_op jit(solution)/shard_map/channelize/pallas_call | solution.py:131
  31.8 7.9 %all-to-all-done = bf16[8,384,128]{2,1,0:T(8,128)(2,1)S(1)} async-done(((bf16[8,384,128]{2,1,0:T(8,128)(2,1)}), bf16[8,384,128]{2,1,0:T(8,128)(2,1)S(1)}, u32[]{:S(2)}, u32[]{:S(2)}) %all-to-all-start) | async-done | bytes 786464 | tf_op jit(solution)/shard_map/all_to_all | solution.py:271
  39.7 3.6 %all-to-all-start.1 = ((bf16[8,192,128]{2,1,0:T(8,128)(2,1)}), bf16[8,192,128]{2,1,0:T(8,128)(2,1)S(1)}, u32[]{:S(2)}, u32[]{:S(2)}) async-start(bf16[8,192,128]{2,1,0:T(8,128)(2,1)} %get-tuple-element.17), calls=%async_computation.1 | async-start | bytes 786432 | tf_op jit(solution)/shard_map/all_to_all | solution.py:271
  43.2 1.5 %collective-permute-start.1 = (bf16[8,384,128]{2,1,0:T(8,128)(2,1)S(1)}, bf16[8,384,128]{2,1,0:T(8,128)(2,1)S(1)}, u32[]{:S(2)}, u32[]{:S(2)}) collective-permute-start(bf16[8,384,128]{2,1,0:T(8,128)(2,1)S(1)} %all-to-all-done), channel_id=1, source_target_pairs={{0,2},{1,3},{2,0},{3,1},{4,6},{5,7},{6,4},{7,5},{8,10},{9,11},{10,... | collective-permute-start | bytes 2359304 | tf_op jit(solution)/shard_map/ppermute | solution.py:274
  44.8 10.3 %all-to-all-done.1 = bf16[8,192,128]{2,1,0:T(8,128)(2,1)S(1)} async-done(((bf16[8,192,128]{2,1,0:T(8,128)(2,1)}), bf16[8,192,128]{2,1,0:T(8,128)(2,1)S(1)}, u32[]{:S(2)}, u32[]{:S(2)}) %all-to-all-start.1) | async-done | bytes 393248 | tf_op jit(solution)/shard_map/all_to_all | solution.py:271
  55.1 3.6 %all-to-all-start.2 = ((bf16[8,192,128]{2,1,0:T(8,128)(2,1)}), bf16[8,192,128]{2,1,0:T(8,128)(2,1)S(1)}, u32[]{:S(2)}, u32[]{:S(2)}) async-start(bf16[8,192,128]{2,1,0:T(8,128)(2,1)} %get-tuple-element.18), calls=%async_computation.2 | async-start | bytes 786432 | tf_op jit(solution)/shard_map/all_to_all | solution.py:271
  58.8 1.6 %collective-permute-start.3 = (bf16[8,192,128]{2,1,0:T(8,128)(2,1)S(1)}, bf16[8,192,128]{2,1,0:T(8,128)(2,1)}, u32[]{:S(2)}, u32[]{:S(2)}) collective-permute-start(bf16[8,192,128]{2,1,0:T(8,128)(2,1)S(1)} %all-to-all-done.1), channel_id=1, source_target_pairs={{0,2},{1,3},{2,0},{3,1},{4,6},{5,7},{6,4},{7,5},{8,10},{9,11},{10,... | collective-permute-start | bytes 1179656 | tf_op jit(solution)/shard_map/ppermute | solution.py:274
  60.3 0.0 collective-permute-start
  60.3 3.4 %collective-permute-done.1 = bf16[8,384,128]{2,1,0:T(8,128)(2,1)S(1)} collective-permute-done((bf16[8,384,128]{2,1,0:T(8,128)(2,1)S(1)}, bf16[8,384,128]{2,1,0:T(8,128)(2,1)S(1)}, u32[]{:S(2)}, u32[]{:S(2)}) %collective-permute-start.1) | collective-permute-done | bytes 786464 | tf_op jit(solution)/shard_map/ppermute | solution.py:274
  63.7 0.0 collective-permute-start.2
  63.7 0.5 collective-permute-start.6
  64.2 6.3 %all-to-all-done.2 = bf16[8,192,128]{2,1,0:T(8,128)(2,1)S(1)} async-done(((bf16[8,192,128]{2,1,0:T(8,128)(2,1)}), bf16[8,192,128]{2,1,0:T(8,128)(2,1)S(1)}, u32[]{:S(2)}, u32[]{:S(2)}) %all-to-all-start.2) | async-done | bytes 393248 | tf_op jit(solution)/shard_map/all_to_all | solution.py:271
  70.5 0.4 collective-permute-done.3
  71.0 0.0 collective-permute-start.7
  71.0 1.5 %collective-permute-start.5 = (bf16[8,192,128]{2,1,0:T(8,128)(2,1)S(1)}, bf16[8,192,128]{2,1,0:T(8,128)(2,1)}, u32[]{:S(2)}, u32[]{:S(2)}) collective-permute-start(bf16[8,192,128]{2,1,0:T(8,128)(2,1)S(1)} %all-to-all-done.2), channel_id=1, source_target_pairs={{0,2},{1,3},{2,0},{3,1},{4,6},{5,7},{6,4},{7,5},{8,10},{9,11},{10,... | collective-permute-start | bytes 1179656 | tf_op jit(solution)/shard_map/ppermute | solution.py:274
  72.5 0.0 collective-permute-done
  72.5 0.2 collective-permute-start.4
  72.7 0.0 collective-permute-done.6
  72.7 0.3 collective-permute-done.7
  73.0 0.0 collective-permute-done.2
  73.0 0.3 copy-done.3
  73.4 0.0 copy-done.5
  73.4 0.0 copy-done.2
  73.4 12.8 %beams.2.rest_8_ = bf16[12,4096,128]{2,1,0:T(8,128)(2,1)} custom-call(s32[1]{0:T(128)} %bitcast.me_ref, bf16[12,8192,128]{2,1,0:T(8,128)(2,1)} %bitcast.26, bf16[8,12,32,128]{3,2,1,0:T(8,128)(2,1)} %bitcast.28, bf16[8,12,32,128]{3,2,1,0:T(8,128)(2,1)} %bitcast.33, bf16[8,12,32,128]{3,2,1,0:T(8,128)(2,1)} %bitcast.31, ...), custom_call_target="tpu_custom_call" | custom-call | flops 12000000000 | bytes 12582912 | tf_op jit(solution)/shard_map/beams/pallas_call | solution.py:214
  86.1 0.0 collective-permute-done.5
  86.1 0.3 collective-permute-start.8
  86.4 0.0 collective-permute-done.4
  86.4 1.7 %collective-permute-done.8 = bf16[8,192,128]{2,1,0:T(8,128)(2,1)S(1)} collective-permute-done((bf16[8,192,128]{2,1,0:T(8,128)(2,1)}, bf16[8,192,128]{2,1,0:T(8,128)(2,1)S(1)}, u32[]{:S(2)}, u32[]{:S(2)}) %collective-permute-start.8) | collective-permute-done | bytes 393248 | tf_op jit(solution)/shard_map/ppermute | solution.py:277
  88.1 0.8 copy-done.4
  88.9 12.8 %beams.3 = bf16[12,4096,128]{2,1,0:T(8,128)(2,1)} custom-call(s32[1]{0:T(128)} %bitcast.me_ref, bf16[12,8192,128]{2,1,0:T(8,128)(2,1)} %bitcast.27, bf16[8,12,32,128]{3,2,1,0:T(8,128)(2,1)} %bitcast.29, bf16[8,12,32,128]{3,2,1,0:T(8,128)(2,1)} %bitcast.34, bf16[8,12,32,128]{3,2,1,0:T(8,128)(2,1)} %bitcast.32, ...), custom_call_target="tpu_custom_call", output_to_operand_aliasing={{}: (10, {})} | custom-call | flops 12000000000 | bytes 12582912 | tf_op jit(solution)/shard_map/beams/pallas_call | solution.py:214
  (8 shorter events, 0.0 us)
Async XLA Ops:
  12.2 27.5 %all-to-all-start = ((bf16[8,384,128]{2,1,0:T(8,128)(2,1)}), bf16[8,384,128]{2,1,0:T(8,128)(2,1)S(1)}, u32[]{:S(2)}, u32[]{:S(2)}) async-start(bf16[8,384,128]{2,1,0:T(8,128)(2,1)} %channelize.2), calls=%async_computation | async-start | bytes 1572864 | tf_op jit(solution)/shard_map/all_to_all | solution.py:271
  39.7 33.7 %copy-start = (bf16[8,384,128]{2,1,0:T(8,128)(2,1)}, bf16[8,384,128]{2,1,0:T(8,128)(2,1)S(1)}, u32[]{:S(2)}) copy-start(bf16[8,384,128]{2,1,0:T(8,128)(2,1)S(1)} %all-to-all-done) | copy-start | bytes 2359300
  39.7 15.4 %all-to-all-start.1 = ((bf16[8,192,128]{2,1,0:T(8,128)(2,1)}), bf16[8,192,128]{2,1,0:T(8,128)(2,1)S(1)}, u32[]{:S(2)}, u32[]{:S(2)}) async-start(bf16[8,192,128]{2,1,0:T(8,128)(2,1)} %get-tuple-element.17), calls=%async_computation.1 | async-start | bytes 786432 | tf_op jit(solution)/shard_map/all_to_all | solution.py:271
  43.2 20.5 %collective-permute-start.1 = (bf16[8,384,128]{2,1,0:T(8,128)(2,1)S(1)}, bf16[8,384,128]{2,1,0:T(8,128)(2,1)S(1)}, u32[]{:S(2)}, u32[]{:S(2)}) collective-permute-start(bf16[8,384,128]{2,1,0:T(8,128)(2,1)S(1)} %all-to-all-done), channel_id=1, source_target_pairs={{0,2},{1,3},{2,0},{3,1},{4,6},{5,7},{6,4},{7,5},{8,10},{9,11},{10,... | collective-permute-start | bytes 2359304 | tf_op jit(solution)/shard_map/ppermute | solution.py:274
  55.1 18.3 %copy-start.5 = (bf16[8,192,128]{2,1,0:T(8,128)(2,1)}, bf16[8,192,128]{2,1,0:T(8,128)(2,1)S(1)}, u32[]{:S(2)}) copy-start(bf16[8,192,128]{2,1,0:T(8,128)(2,1)S(1)} %all-to-all-done.1) | copy-start | bytes 1179652
  55.1 15.4 %all-to-all-start.2 = ((bf16[8,192,128]{2,1,0:T(8,128)(2,1)}), bf16[8,192,128]{2,1,0:T(8,128)(2,1)S(1)}, u32[]{:S(2)}, u32[]{:S(2)}) async-start(bf16[8,192,128]{2,1,0:T(8,128)(2,1)} %get-tuple-element.18), calls=%async_computation.2 | async-start | bytes 786432 | tf_op jit(solution)/shard_map/all_to_all | solution.py:271
  58.8 12.2 %collective-permute-start.3 = (bf16[8,192,128]{2,1,0:T(8,128)(2,1)S(1)}, bf16[8,192,128]{2,1,0:T(8,128)(2,1)}, u32[]{:S(2)}, u32[]{:S(2)}) collective-permute-start(bf16[8,192,128]{2,1,0:T(8,128)(2,1)S(1)} %all-to-all-done.1), channel_id=1, source_target_pairs={{0,2},{1,3},{2,0},{3,1},{4,6},{5,7},{6,4},{7,5},{8,10},{9,11},{10,... | collective-permute-start | bytes 1179656 | tf_op jit(solution)/shard_map/ppermute | solution.py:274
  60.3 12.2 %collective-permute-start = (bf16[8,384,128]{2,1,0:T(8,128)(2,1)S(1)}, bf16[8,384,128]{2,1,0:T(8,128)(2,1)S(1)}, u32[]{:S(2)}, u32[]{:S(2)}) collective-permute-start(bf16[8,384,128]{2,1,0:T(8,128)(2,1)S(1)} %all-to-all-done), channel_id=1, source_target_pairs={{0,1},{1,0},{2,3},{3,2},{4,5},{5,4},{6,7},{7,6},{8,9},{9,8},{10,11... | collective-permute-start | bytes 2359304 | tf_op jit(solution)/shard_map/ppermute | solution.py:277
  63.7 9.7 %copy-start.2 = (bf16[8,384,128]{2,1,0:T(8,128)(2,1)}, bf16[8,384,128]{2,1,0:T(8,128)(2,1)S(1)}, u32[]{:S(2)}) copy-start(bf16[8,384,128]{2,1,0:T(8,128)(2,1)S(1)} %collective-permute-done.1) | copy-start | bytes 2359300
  63.7 9.3 %collective-permute-start.2 = (bf16[8,384,128]{2,1,0:T(8,128)(2,1)S(1)}, bf16[8,384,128]{2,1,0:T(8,128)(2,1)}, u32[]{:S(2)}, u32[]{:S(2)}) collective-permute-start(bf16[8,384,128]{2,1,0:T(8,128)(2,1)S(1)} %collective-permute-done.1), channel_id=1, source_target_pairs={{0,1},{1,0},{2,3},{3,2},{4,5},{5,4},{6,7},{7,6},{8,9},{9,8},{10,11... | collective-permute-start | bytes 2359304 | tf_op jit(solution)/shard_map/ppermute | solution.py:277
  63.7 9.0 %collective-permute-start.6 = (bf16[8,192,128]{2,1,0:T(8,128)(2,1)S(1)}, bf16[8,192,128]{2,1,0:T(8,128)(2,1)}, u32[]{:S(2)}, u32[]{:S(2)}) collective-permute-start(bf16[8,192,128]{2,1,0:T(8,128)(2,1)S(1)} %all-to-all-done.1), channel_id=1, source_target_pairs={{0,1},{1,0},{2,3},{3,2},{4,5},{5,4},{6,7},{7,6},{8,9},{9,8},{10,11... | collective-permute-start | bytes 1179656 | tf_op jit(solution)/shard_map/ppermute | solution.py:277
  70.5 15.6 %copy-start.1 = (bf16[8,192,128]{2,1,0:T(8,128)(2,1)}, bf16[8,192,128]{2,1,0:T(8,128)(2,1)S(1)}, u32[]{:S(2)}) copy-start(bf16[8,192,128]{2,1,0:T(8,128)(2,1)S(1)} %all-to-all-done.2) | copy-start | bytes 1179652
  71.0 2.1 %collective-permute-start.7 = (bf16[8,192,128]{2,1,0:T(8,128)(2,1)}, bf16[8,192,128]{2,1,0:T(8,128)(2,1)}, u32[]{:S(2)}, u32[]{:S(2)}) collective-permute-start(bf16[8,192,128]{2,1,0:T(8,128)(2,1)} %collective-permute-done.3), channel_id=1, source_target_pairs={{0,1},{1,0},{2,3},{3,2},{4,5},{5,4},{6,7},{7,6},{8,9},{9,8},{10,11... | collective-permute-start | bytes 1179656 | tf_op jit(solution)/shard_map/ppermute | solution.py:277
  71.0 15.2 %collective-permute-start.5 = (bf16[8,192,128]{2,1,0:T(8,128)(2,1)S(1)}, bf16[8,192,128]{2,1,0:T(8,128)(2,1)}, u32[]{:S(2)}, u32[]{:S(2)}) collective-permute-start(bf16[8,192,128]{2,1,0:T(8,128)(2,1)S(1)} %all-to-all-done.2), channel_id=1, source_target_pairs={{0,2},{1,3},{2,0},{3,1},{4,6},{5,7},{6,4},{7,5},{8,10},{9,11},{10,... | collective-permute-start | bytes 1179656 | tf_op jit(solution)/shard_map/ppermute | solution.py:274
  72.5 0.9 copy-start.3
  72.5 14.0 %collective-permute-start.4 = (bf16[8,192,128]{2,1,0:T(8,128)(2,1)S(1)}, bf16[8,192,128]{2,1,0:T(8,128)(2,1)}, u32[]{:S(2)}, u32[]{:S(2)}) collective-permute-start(bf16[8,192,128]{2,1,0:T(8,128)(2,1)S(1)} %all-to-all-done.2), channel_id=1, source_target_pairs={{0,1},{1,0},{2,3},{3,2},{4,5},{5,4},{6,7},{7,6},{8,9},{9,8},{10,11... | collective-permute-start | bytes 1179656 | tf_op jit(solution)/shard_map/ppermute | solution.py:277
  86.1 2.0 %collective-permute-start.8 = (bf16[8,192,128]{2,1,0:T(8,128)(2,1)}, bf16[8,192,128]{2,1,0:T(8,128)(2,1)S(1)}, u32[]{:S(2)}, u32[]{:S(2)}) collective-permute-start(bf16[8,192,128]{2,1,0:T(8,128)(2,1)} %collective-permute-done.5), channel_id=1, source_target_pairs={{0,1},{1,0},{2,3},{3,2},{4,5},{5,4},{6,7},{7,6},{8,9},{9,8},{10,11... | collective-permute-start | bytes 1179656 | tf_op jit(solution)/shard_map/ppermute | solution.py:277
  88.1 0.8 copy-start.4

commit v5 on v4

--- a/solution.py
+++ b/solution.py
@@ -231,7 +231,7 @@
             pltpu.VMEM((sub, (tile + 8) * pr, m), jnp.float32),
         ],
         input_output_aliases={len(operands) - 1: 0} if aliased else {},
-        compiler_params=pltpu.CompilerParams(vmem_limit_bytes=62 << 20),
+        compiler_params=pltpu.CompilerParams(vmem_limit_bytes=40 << 20),
         cost_estimate=pl.CostEstimate(
             flops=24 * 10**9 * count // 12, bytes_accessed=count * rows * 256, transcendentals=0
         ),

time: 102 us -> 99.9 us (0.979)
  local copies, waits for them, and re-layouts: 1.09 us -> 0 us
    unnamed x12 -> x0, local copies, waits for them, and re-layouts: 1.09 us -> none
where the time goes in v5:
time: 99.9 us; the launch traced here: 99.5 us
  Pallas kernels  49.2 us (49%)
  waiting for transfers between devices  30.3 us (30%)
  starting transfers between devices  19.9 us (20%)
    pallas_call x2, Pallas kernels, form_beams(): pl.pallas_call(functools.partial(beam_kernel, (sub, pr, halves, groups, i...  24.7 us
    all_to_all x3, waiting for transfers between devices, turn(): return lax.all_to_all(part, 'chan', split_axis=0, concat_axis=0, tiled=True)  24.6 us
    pallas_call x2, Pallas kernels, channelize(): pl.pallas_call(functools.partial(channelize_kernel, dims), grid=(stations...  24.5 us
    all_to_all x3, starting transfers between devices, turn(): return lax.all_to_all(part, 'chan', split_axis=0, concat_axis=0, tiled=True)  14.5 us
    ppermute x3, starting transfers between devices, far(): lax.ppermute(part, 'grp', [(g, g ^ d) for g in range(groups)])  4.57 us
    ppermute x3, waiting for transfers between devices, far(): lax.ppermute(part, 'grp', [(g, g ^ d) for g in range(groups)])  3.83 us
  transfers between devices with their start and end apart: 12, of which 7 were waited for; matrix products, arithmetic and copies ran while one was open for 0% of the time, Pallas kernels for 25%

profile of v5, /device:TPU:0, one launch (start us, length us, event | category | flops | bytes accessed | tf_op | source)
XLA Modules:
  0.0 99.5 jit_solution(1933587955573267832)
XLA Ops:
  0.0 12.2 %channelize.2 = bf16[8,384,128]{2,1,0:T(8,128)(2,1)} custom-call(bf16[16,2224,128]{2,1,0:T(8,128)(2,1)} %bitcast.39, f32[12,512]{1,0:T(8,128)} %t_ref.3, s32[96]{0:T(128)} %chan_ref.3), custom_call_target="tpu_custom_call" | custom-call | flops 7000000000 | bytes 4554752 | tf_op jit(solution)/shard_map/channelize/pallas_call | solution.py:131
  12.2 7.3 %all-to-all-start = ((bf16[8,384,128]{2,1,0:T(8,128)(2,1)}), bf16[8,384,128]{2,1,0:T(8,128)(2,1)S(1)}, u32[]{:S(2)}, u32[]{:S(2)}) async-start(bf16[8,384,128]{2,1,0:T(8,128)(2,1)} %channelize.2), calls=%async_computation | async-start | bytes 1572864 | tf_op jit(solution)/shard_map/all_to_all | solution.py:271
  19.5 12.3 %channelize.3 = (bf16[8,192,128]{2,1,0:T(8,128)(2,1)}, bf16[8,192,128]{2,1,0:T(8,128)(2,1)}) custom-call(bf16[16,2224,128]{2,1,0:T(8,128)(2,1)} %bitcast.40, f32[12,512]{1,0:T(8,128)} %t_ref.3, s32[96]{0:T(128)} %chan_ref.3), custom_call_target="tpu_custom_call" | custom-call | flops 7000000000 | bytes 4554752 | tf_op jit(solution)/shard_map/channelize/pallas_call | solution.py:131
  31.8 7.9 %all-to-all-done = bf16[8,384,128]{2,1,0:T(8,128)(2,1)S(1)} async-done(((bf16[8,384,128]{2,1,0:T(8,128)(2,1)}), bf16[8,384,128]{2,1,0:T(8,128)(2,1)S(1)}, u32[]{:S(2)}, u32[]{:S(2)}) %all-to-all-start) | async-done | bytes 786464 | tf_op jit(solution)/shard_map/all_to_all | solution.py:271
  39.7 3.6 %all-to-all-start.1 = ((bf16[8,192,128]{2,1,0:T(8,128)(2,1)}), bf16[8,192,128]{2,1,0:T(8,128)(2,1)S(1)}, u32[]{:S(2)}, u32[]{:S(2)}) async-start(bf16[8,192,128]{2,1,0:T(8,128)(2,1)} %get-tuple-element.17), calls=%async_computation.1 | async-start | bytes 786432 | tf_op jit(solution)/shard_map/all_to_all | solution.py:271
  43.2 1.5 %collective-permute-start.1 = (bf16[8,384,128]{2,1,0:T(8,128)(2,1)S(1)}, bf16[8,384,128]{2,1,0:T(8,128)(2,1)S(1)}, u32[]{:S(2)}, u32[]{:S(2)}) collective-permute-start(bf16[8,384,128]{2,1,0:T(8,128)(2,1)S(1)} %all-to-all-done), channel_id=1, source_target_pairs={{0,2},{1,3},{2,0},{3,1},{4,6},{5,7},{6,4},{7,5},{8,10},{9,11},{10,... | collective-permute-start | bytes 2359304 | tf_op jit(solution)/shard_map/ppermute | solution.py:274
  44.8 10.3 %all-to-all-done.1 = bf16[8,192,128]{2,1,0:T(8,128)(2,1)S(1)} async-done(((bf16[8,192,128]{2,1,0:T(8,128)(2,1)}), bf16[8,192,128]{2,1,0:T(8,128)(2,1)S(1)}, u32[]{:S(2)}, u32[]{:S(2)}) %all-to-all-start.1) | async-done | bytes 393248 | tf_op jit(solution)/shard_map/all_to_all | solution.py:271
  55.1 3.6 %all-to-all-start.2 = ((bf16[8,192,128]{2,1,0:T(8,128)(2,1)}), bf16[8,192,128]{2,1,0:T(8,128)(2,1)S(1)}, u32[]{:S(2)}, u32[]{:S(2)}) async-start(bf16[8,192,128]{2,1,0:T(8,128)(2,1)} %get-tuple-element.18), calls=%async_computation.2 | async-start | bytes 786432 | tf_op jit(solution)/shard_map/all_to_all | solution.py:271
  58.7 1.6 %collective-permute-start.3 = (bf16[8,192,128]{2,1,0:T(8,128)(2,1)S(1)}, bf16[8,192,128]{2,1,0:T(8,128)(2,1)}, u32[]{:S(2)}, u32[]{:S(2)}) collective-permute-start(bf16[8,192,128]{2,1,0:T(8,128)(2,1)S(1)} %all-to-all-done.1), channel_id=1, source_target_pairs={{0,2},{1,3},{2,0},{3,1},{4,6},{5,7},{6,4},{7,5},{8,10},{9,11},{10,... | collective-permute-start | bytes 1179656 | tf_op jit(solution)/shard_map/ppermute | solution.py:274
  60.3 0.0 collective-permute-start
  60.3 3.4 %collective-permute-done.1 = bf16[8,384,128]{2,1,0:T(8,128)(2,1)S(1)} collective-permute-done((bf16[8,384,128]{2,1,0:T(8,128)(2,1)S(1)}, bf16[8,384,128]{2,1,0:T(8,128)(2,1)S(1)}, u32[]{:S(2)}, u32[]{:S(2)}) %collective-permute-start.1) | collective-permute-done | bytes 786464 | tf_op jit(solution)/shard_map/ppermute | solution.py:274
  63.7 0.0 collective-permute-start.2
  63.7 0.5 collective-permute-start.6
  64.2 6.3 %all-to-all-done.2 = bf16[8,192,128]{2,1,0:T(8,128)(2,1)S(1)} async-done(((bf16[8,192,128]{2,1,0:T(8,128)(2,1)}), bf16[8,192,128]{2,1,0:T(8,128)(2,1)S(1)}, u32[]{:S(2)}, u32[]{:S(2)}) %all-to-all-start.2) | async-done | bytes 393248 | tf_op jit(solution)/shard_map/all_to_all | solution.py:271
  70.5 0.4 collective-permute-done.3
  71.0 0.0 collective-permute-start.7
  71.0 1.5 %collective-permute-start.5 = (bf16[8,192,128]{2,1,0:T(8,128)(2,1)S(1)}, bf16[8,192,128]{2,1,0:T(8,128)(2,1)S(1)}, u32[]{:S(2)}, u32[]{:S(2)}) collective-permute-start(bf16[8,192,128]{2,1,0:T(8,128)(2,1)S(1)} %all-to-all-done.2), channel_id=1, source_target_pairs={{0,2},{1,3},{2,0},{3,1},{4,6},{5,7},{6,4},{7,5},{8,10},{9,11},{10,... | collective-permute-start | bytes 1179656 | tf_op jit(solution)/shard_map/ppermute | solution.py:274
  72.5 0.0 collective-permute-done
  72.5 0.2 collective-permute-start.4
  72.7 0.0 collective-permute-done.6
  72.7 0.3 collective-permute-done.7
  73.0 0.0 collective-permute-done.2
  73.0 12.4 %beams.2.rest_8_ = bf16[12,4096,128]{2,1,0:T(8,128)(2,1)} custom-call(s32[1]{0:T(128)} %bitcast.me_ref, bf16[12,8192,128]{2,1,0:T(8,128)(2,1)} %bitcast.37, bf16[8,12,32,128]{3,2,1,0:T(8,128)(2,1)S(1)} %bitcast.26, bf16[8,12,32,128]{3,2,1,0:T(8,128)(2,1)S(1)} %bitcast.31, bf16[8,12,32,128]{3,2,1,0:T(8,128)(2,1)S(1)} %bitcast.29, ...), custom_call_target="tpu_custom_call" | custom-call | flops 12000000000 | bytes 12582912 | tf_op jit(solution)/shard_map/beams/pallas_call | solution.py:214
  85.5 0.0 collective-permute-done.5
  85.5 0.1 collective-permute-start.8
  85.6 0.0 collective-permute-done.4
  85.6 1.6 %collective-permute-done.8 = bf16[8,192,128]{2,1,0:T(8,128)(2,1)S(1)} collective-permute-done((bf16[8,192,128]{2,1,0:T(8,128)(2,1)S(1)}, bf16[8,192,128]{2,1,0:T(8,128)(2,1)S(1)}, u32[]{:S(2)}, u32[]{:S(2)}) %collective-permute-start.8) | collective-permute-done | bytes 393248 | tf_op jit(solution)/shard_map/ppermute | solution.py:277
  87.2 12.3 %beams.3 = bf16[12,4096,128]{2,1,0:T(8,128)(2,1)} custom-call(s32[1]{0:T(128)} %bitcast.me_ref, bf16[12,8192,128]{2,1,0:T(8,128)(2,1)} %bitcast.38, bf16[8,12,32,128]{3,2,1,0:T(8,128)(2,1)S(1)} %bitcast.27, bf16[8,12,32,128]{3,2,1,0:T(8,128)(2,1)S(1)} %bitcast.32, bf16[8,12,32,128]{3,2,1,0:T(8,128)(2,1)S(1)} %bitcast.30, ...), custom_call_target="tpu_custom_call", output_to_operand_aliasing={{}: (10, {})} | custom-call | flops 12000000000 | bytes 12582912 | tf_op jit(solution)/shard_map/beams/pallas_call | solution.py:214
Async XLA Ops:
  12.2 27.5 %all-to-all-start = ((bf16[8,384,128]{2,1,0:T(8,128)(2,1)}), bf16[8,384,128]{2,1,0:T(8,128)(2,1)S(1)}, u32[]{:S(2)}, u32[]{:S(2)}) async-start(bf16[8,384,128]{2,1,0:T(8,128)(2,1)} %channelize.2), calls=%async_computation | async-start | bytes 1572864 | tf_op jit(solution)/shard_map/all_to_all | solution.py:271
  39.7 15.4 %all-to-all-start.1 = ((bf16[8,192,128]{2,1,0:T(8,128)(2,1)}), bf16[8,192,128]{2,1,0:T(8,128)(2,1)S(1)}, u32[]{:S(2)}, u32[]{:S(2)}) async-start(bf16[8,192,128]{2,1,0:T(8,128)(2,1)} %get-tuple-element.17), calls=%async_computation.1 | async-start | bytes 786432 | tf_op jit(solution)/shard_map/all_to_all | solution.py:271
  43.2 20.5 %collective-permute-start.1 = (bf16[8,384,128]{2,1,0:T(8,128)(2,1)S(1)}, bf16[8,384,128]{2,1,0:T(8,128)(2,1)S(1)}, u32[]{:S(2)}, u32[]{:S(2)}) collective-permute-start(bf16[8,384,128]{2,1,0:T(8,128)(2,1)S(1)} %all-to-all-done), channel_id=1, source_target_pairs={{0,2},{1,3},{2,0},{3,1},{4,6},{5,7},{6,4},{7,5},{8,10},{9,11},{10,... | collective-permute-start | bytes 2359304 | tf_op jit(solution)/shard_map/ppermute | solution.py:274
  55.1 15.4 %all-to-all-start.2 = ((bf16[8,192,128]{2,1,0:T(8,128)(2,1)}), bf16[8,192,128]{2,1,0:T(8,128)(2,1)S(1)}, u32[]{:S(2)}, u32[]{:S(2)}) async-start(bf16[8,192,128]{2,1,0:T(8,128)(2,1)} %get-tuple-element.18), calls=%async_computation.2 | async-start | bytes 786432 | tf_op jit(solution)/shard_map/all_to_all | solution.py:271
  58.7 12.2 %collective-permute-start.3 = (bf16[8,192,128]{2,1,0:T(8,128)(2,1)S(1)}, bf16[8,192,128]{2,1,0:T(8,128)(2,1)}, u32[]{:S(2)}, u32[]{:S(2)}) collective-permute-start(bf16[8,192,128]{2,1,0:T(8,128)(2,1)S(1)} %all-to-all-done.1), channel_id=1, source_target_pairs={{0,2},{1,3},{2,0},{3,1},{4,6},{5,7},{6,4},{7,5},{8,10},{9,11},{10,... | collective-permute-start | bytes 1179656 | tf_op jit(solution)/shard_map/ppermute | solution.py:274
  60.3 12.2 %collective-permute-start = (bf16[8,384,128]{2,1,0:T(8,128)(2,1)S(1)}, bf16[8,384,128]{2,1,0:T(8,128)(2,1)S(1)}, u32[]{:S(2)}, u32[]{:S(2)}) collective-permute-start(bf16[8,384,128]{2,1,0:T(8,128)(2,1)S(1)} %all-to-all-done), channel_id=1, source_target_pairs={{0,1},{1,0},{2,3},{3,2},{4,5},{5,4},{6,7},{7,6},{8,9},{9,8},{10,11... | collective-permute-start | bytes 2359304 | tf_op jit(solution)/shard_map/ppermute | solution.py:277
  63.7 9.3 %collective-permute-start.2 = (bf16[8,384,128]{2,1,0:T(8,128)(2,1)S(1)}, bf16[8,384,128]{2,1,0:T(8,128)(2,1)}, u32[]{:S(2)}, u32[]{:S(2)}) collective-permute-start(bf16[8,384,128]{2,1,0:T(8,128)(2,1)S(1)} %collective-permute-done.1), channel_id=1, source_target_pairs={{0,1},{1,0},{2,3},{3,2},{4,5},{5,4},{6,7},{7,6},{8,9},{9,8},{10,11... | collective-permute-start | bytes 2359304 | tf_op jit(solution)/shard_map/ppermute | solution.py:277
  63.7 9.0 %collective-permute-start.6 = (bf16[8,192,128]{2,1,0:T(8,128)(2,1)S(1)}, bf16[8,192,128]{2,1,0:T(8,128)(2,1)}, u32[]{:S(2)}, u32[]{:S(2)}) collective-permute-start(bf16[8,192,128]{2,1,0:T(8,128)(2,1)S(1)} %all-to-all-done.1), channel_id=1, source_target_pairs={{0,1},{1,0},{2,3},{3,2},{4,5},{5,4},{6,7},{7,6},{8,9},{9,8},{10,11... | collective-permute-start | bytes 1179656 | tf_op jit(solution)/shard_map/ppermute | solution.py:277
  71.0 2.1 %collective-permute-start.7 = (bf16[8,192,128]{2,1,0:T(8,128)(2,1)}, bf16[8,192,128]{2,1,0:T(8,128)(2,1)}, u32[]{:S(2)}, u32[]{:S(2)}) collective-permute-start(bf16[8,192,128]{2,1,0:T(8,128)(2,1)} %collective-permute-done.3), channel_id=1, source_target_pairs={{0,1},{1,0},{2,3},{3,2},{4,5},{5,4},{6,7},{7,6},{8,9},{9,8},{10,11... | collective-permute-start | bytes 1179656 | tf_op jit(solution)/shard_map/ppermute | solution.py:277
  71.0 14.5 %collective-permute-start.5 = (bf16[8,192,128]{2,1,0:T(8,128)(2,1)S(1)}, bf16[8,192,128]{2,1,0:T(8,128)(2,1)S(1)}, u32[]{:S(2)}, u32[]{:S(2)}) collective-permute-start(bf16[8,192,128]{2,1,0:T(8,128)(2,1)S(1)} %all-to-all-done.2), channel_id=1, source_target_pairs={{0,2},{1,3},{2,0},{3,1},{4,6},{5,7},{6,4},{7,5},{8,10},{9,11},{10,... | collective-permute-start | bytes 1179656 | tf_op jit(solution)/shard_map/ppermute | solution.py:274
  72.5 13.1 %collective-permute-start.4 = (bf16[8,192,128]{2,1,0:T(8,128)(2,1)S(1)}, bf16[8,192,128]{2,1,0:T(8,128)(2,1)S(1)}, u32[]{:S(2)}, u32[]{:S(2)}) collective-permute-start(bf16[8,192,128]{2,1,0:T(8,128)(2,1)S(1)} %all-to-all-done.2), channel_id=1, source_target_pairs={{0,1},{1,0},{2,3},{3,2},{4,5},{5,4},{6,7},{7,6},{8,9},{9,8},{10,11... | collective-permute-start | bytes 1179656 | tf_op jit(solution)/shard_map/ppermute | solution.py:277
  85.5 1.7 %collective-permute-start.8 = (bf16[8,192,128]{2,1,0:T(8,128)(2,1)S(1)}, bf16[8,192,128]{2,1,0:T(8,128)(2,1)S(1)}, u32[]{:S(2)}, u32[]{:S(2)}) collective-permute-start(bf16[8,192,128]{2,1,0:T(8,128)(2,1)S(1)} %collective-permute-done.5), channel_id=1, source_target_pairs={{0,1},{1,0},{2,3},{3,2},{4,5},{5,4},{6,7},{7,6},{8,9},{9,8},{10,11... | collective-permute-start | bytes 1179656 | tf_op jit(solution)/shard_map/ppermute | solution.py:277

commit v6 on v5

--- a/solution.py
+++ b/solution.py
@@ -231,7 +231,7 @@
             pltpu.VMEM((sub, (tile + 8) * pr, m), jnp.float32),
         ],
         input_output_aliases={len(operands) - 1: 0} if aliased else {},
-        compiler_params=pltpu.CompilerParams(vmem_limit_bytes=40 << 20),
+        compiler_params=pltpu.CompilerParams(vmem_limit_bytes=30 << 20),
         cost_estimate=pl.CostEstimate(
             flops=24 * 10**9 * count // 12, bytes_accessed=count * rows * 256, transcendentals=0
         ),

time: 99.9 us -> 99.9 us (level)
  no operation moved by 1% of the time
where the time goes in v6:
time: 99.9 us; the launch traced here: 99.5 us
  Pallas kernels  49.2 us (49%)
  waiting for transfers between devices  30.3 us (30%)
  starting transfers between devices  19.9 us (20%)
    pallas_call x2, Pallas kernels, form_beams(): pl.pallas_call(functools.partial(beam_kernel, (sub, pr, halves, groups, i...  24.7 us
    all_to_all x3, waiting for transfers between devices, turn(): return lax.all_to_all(part, 'chan', split_axis=0, concat_axis=0, tiled=True)  24.6 us
    pallas_call x2, Pallas kernels, channelize(): pl.pallas_call(functools.partial(channelize_kernel, dims), grid=(stations...  24.5 us
    all_to_all x3, starting transfers between devices, turn(): return lax.all_to_all(part, 'chan', split_axis=0, concat_axis=0, tiled=True)  14.5 us
    ppermute x3, starting transfers between devices, far(): lax.ppermute(part, 'grp', [(g, g ^ d) for g in range(groups)])  4.57 us
    ppermute x3, waiting for transfers between devices, far(): lax.ppermute(part, 'grp', [(g, g ^ d) for g in range(groups)])  3.83 us
  transfers between devices with their start and end apart: 12, of which 7 were waited for; matrix products, arithmetic and copies ran while one was open for 0% of the time, Pallas kernels for 25%

profile of v6, /device:TPU:0, one launch (start us, length us, event | category | flops | bytes accessed | tf_op | source)
XLA Modules:
  0.0 99.5 jit_solution(3477477708033126941)
XLA Ops:
  0.0 12.2 %channelize.2 = bf16[8,384,128]{2,1,0:T(8,128)(2,1)} custom-call(bf16[16,2224,128]{2,1,0:T(8,128)(2,1)} %bitcast.39, f32[12,512]{1,0:T(8,128)} %t_ref.3, s32[96]{0:T(128)} %chan_ref.3), custom_call_target="tpu_custom_call" | custom-call | flops 7000000000 | bytes 4554752 | tf_op jit(solution)/shard_map/channelize/pallas_call | solution.py:131
  12.2 7.3 %all-to-all-start = ((bf16[8,384,128]{2,1,0:T(8,128)(2,1)}), bf16[8,384,128]{2,1,0:T(8,128)(2,1)S(1)}, u32[]{:S(2)}, u32[]{:S(2)}) async-start(bf16[8,384,128]{2,1,0:T(8,128)(2,1)} %channelize.2), calls=%async_computation | async-start | bytes 1572864 | tf_op jit(solution)/shard_map/all_to_all | solution.py:271
  19.5 12.3 %channelize.3 = (bf16[8,192,128]{2,1,0:T(8,128)(2,1)}, bf16[8,192,128]{2,1,0:T(8,128)(2,1)}) custom-call(bf16[16,2224,128]{2,1,0:T(8,128)(2,1)} %bitcast.40, f32[12,512]{1,0:T(8,128)} %t_ref.3, s32[96]{0:T(128)} %chan_ref.3), custom_call_target="tpu_custom_call" | custom-call | flops 7000000000 | bytes 4554752 | tf_op jit(solution)/shard_map/channelize/pallas_call | solution.py:131
  31.8 7.9 %all-to-all-done = bf16[8,384,128]{2,1,0:T(8,128)(2,1)S(1)} async-done(((bf16[8,384,128]{2,1,0:T(8,128)(2,1)}), bf16[8,384,128]{2,1,0:T(8,128)(2,1)S(1)}, u32[]{:S(2)}, u32[]{:S(2)}) %all-to-all-start) | async-done | bytes 786464 | tf_op jit(solution)/shard_map/all_to_all | solution.py:271
  39.7 3.6 %all-to-all-start.1 = ((bf16[8,192,128]{2,1,0:T(8,128)(2,1)}), bf16[8,192,128]{2,1,0:T(8,128)(2,1)S(1)}, u32[]{:S(2)}, u32[]{:S(2)}) async-start(bf16[8,192,128]{2,1,0:T(8,128)(2,1)} %get-tuple-element.17), calls=%async_computation.1 | async-start | bytes 786432 | tf_op jit(solution)/shard_map/all_to_all | solution.py:271
  43.2 1.5 %collective-permute-start.1 = (bf16[8,384,128]{2,1,0:T(8,128)(2,1)S(1)}, bf16[8,384,128]{2,1,0:T(8,128)(2,1)S(1)}, u32[]{:S(2)}, u32[]{:S(2)}) collective-permute-start(bf16[8,384,128]{2,1,0:T(8,128)(2,1)S(1)} %all-to-all-done), channel_id=1, source_target_pairs={{0,2},{1,3},{2,0},{3,1},{4,6},{5,7},{6,4},{7,5},{8,10},{9,11},{10,... | collective-permute-start | bytes 2359304 | tf_op jit(solution)/shard_map/ppermute | solution.py:274
  44.8 10.3 %all-to-all-done.1 = bf16[8,192,128]{2,1,0:T(8,128)(2,1)S(1)} async-done(((bf16[8,192,128]{2,1,0:T(8,128)(2,1)}), bf16[8,192,128]{2,1,0:T(8,128)(2,1)S(1)}, u32[]{:S(2)}, u32[]{:S(2)}) %all-to-all-start.1) | async-done | bytes 393248 | tf_op jit(solution)/shard_map/all_to_all | solution.py:271
  55.1 3.6 %all-to-all-start.2 = ((bf16[8,192,128]{2,1,0:T(8,128)(2,1)}), bf16[8,192,128]{2,1,0:T(8,128)(2,1)S(1)}, u32[]{:S(2)}, u32[]{:S(2)}) async-start(bf16[8,192,128]{2,1,0:T(8,128)(2,1)} %get-tuple-element.18), calls=%async_computation.2 | async-start | bytes 786432 | tf_op jit(solution)/shard_map/all_to_all | solution.py:271
  58.7 1.6 %collective-permute-start.3 = (bf16[8,192,128]{2,1,0:T(8,128)(2,1)S(1)}, bf16[8,192,128]{2,1,0:T(8,128)(2,1)}, u32[]{:S(2)}, u32[]{:S(2)}) collective-permute-start(bf16[8,192,128]{2,1,0:T(8,128)(2,1)S(1)} %all-to-all-done.1), channel_id=1, source_target_pairs={{0,2},{1,3},{2,0},{3,1},{4,6},{5,7},{6,4},{7,5},{8,10},{9,11},{10,... | collective-permute-start | bytes 1179656 | tf_op jit(solution)/shard_map/ppermute | solution.py:274
  60.3 0.0 collective-permute-start
  60.3 3.4 %collective-permute-done.1 = bf16[8,384,128]{2,1,0:T(8,128)(2,1)S(1)} collective-permute-done((bf16[8,384,128]{2,1,0:T(8,128)(2,1)S(1)}, bf16[8,384,128]{2,1,0:T(8,128)(2,1)S(1)}, u32[]{:S(2)}, u32[]{:S(2)}) %collective-permute-start.1) | collective-permute-done | bytes 786464 | tf_op jit(solution)/shard_map/ppermute | solution.py:274
  63.7 0.0 collective-permute-start.2
  63.7 0.5 collective-permute-start.6
  64.2 6.3 %all-to-all-done.2 = bf16[8,192,128]{2,1,0:T(8,128)(2,1)S(1)} async-done(((bf16[8,192,128]{2,1,0:T(8,128)(2,1)}), bf16[8,192,128]{2,1,0:T(8,128)(2,1)S(1)}, u32[]{:S(2)}, u32[]{:S(2)}) %all-to-all-start.2) | async-done | bytes 393248 | tf_op jit(solution)/shard_map/all_to_all | solution.py:271
  70.5 0.4 collective-permute-done.3
  71.0 0.0 collective-permute-start.7
  71.0 1.5 %collective-permute-start.5 = (bf16[8,192,128]{2,1,0:T(8,128)(2,1)S(1)}, bf16[8,192,128]{2,1,0:T(8,128)(2,1)S(1)}, u32[]{:S(2)}, u32[]{:S(2)}) collective-permute-start(bf16[8,192,128]{2,1,0:T(8,128)(2,1)S(1)} %all-to-all-done.2), channel_id=1, source_target_pairs={{0,2},{1,3},{2,0},{3,1},{4,6},{5,7},{6,4},{7,5},{8,10},{9,11},{10,... | collective-permute-start | bytes 1179656 | tf_op jit(solution)/shard_map/ppermute | solution.py:274
  72.5 0.0 collective-permute-done
  72.5 0.2 collective-permute-start.4
  72.7 0.0 collective-permute-done.6
  72.7 0.3 collective-permute-done.7
  73.0 0.0 collective-permute-done.2
  73.0 12.4 %beams.2.rest_8_ = bf16[12,4096,128]{2,1,0:T(8,128)(2,1)} custom-call(s32[1]{0:T(128)} %bitcast.me_ref, bf16[12,8192,128]{2,1,0:T(8,128)(2,1)} %bitcast.37, bf16[8,12,32,128]{3,2,1,0:T(8,128)(2,1)S(1)} %bitcast.26, bf16[8,12,32,128]{3,2,1,0:T(8,128)(2,1)S(1)} %bitcast.31, bf16[8,12,32,128]{3,2,1,0:T(8,128)(2,1)S(1)} %bitcast.29, ...), custom_call_target="tpu_custom_call" | custom-call | flops 12000000000 | bytes 12582912 | tf_op jit(solution)/shard_map/beams/pallas_call | solution.py:214
  85.5 0.0 collective-permute-done.5
  85.5 0.1 collective-permute-start.8
  85.6 0.0 collective-permute-done.4
  85.6 1.6 %collective-permute-done.8 = bf16[8,192,128]{2,1,0:T(8,128)(2,1)S(1)} collective-permute-done((bf16[8,192,128]{2,1,0:T(8,128)(2,1)S(1)}, bf16[8,192,128]{2,1,0:T(8,128)(2,1)S(1)}, u32[]{:S(2)}, u32[]{:S(2)}) %collective-permute-start.8) | collective-permute-done | bytes 393248 | tf_op jit(solution)/shard_map/ppermute | solution.py:277
  87.2 12.3 %beams.3 = bf16[12,4096,128]{2,1,0:T(8,128)(2,1)} custom-call(s32[1]{0:T(128)} %bitcast.me_ref, bf16[12,8192,128]{2,1,0:T(8,128)(2,1)} %bitcast.38, bf16[8,12,32,128]{3,2,1,0:T(8,128)(2,1)S(1)} %bitcast.27, bf16[8,12,32,128]{3,2,1,0:T(8,128)(2,1)S(1)} %bitcast.32, bf16[8,12,32,128]{3,2,1,0:T(8,128)(2,1)S(1)} %bitcast.30, ...), custom_call_target="tpu_custom_call", output_to_operand_aliasing={{}: (10, {})} | custom-call | flops 12000000000 | bytes 12582912 | tf_op jit(solution)/shard_map/beams/pallas_call | solution.py:214
Async XLA Ops:
  12.2 27.5 %all-to-all-start = ((bf16[8,384,128]{2,1,0:T(8,128)(2,1)}), bf16[8,384,128]{2,1,0:T(8,128)(2,1)S(1)}, u32[]{:S(2)}, u32[]{:S(2)}) async-start(bf16[8,384,128]{2,1,0:T(8,128)(2,1)} %channelize.2), calls=%async_computation | async-start | bytes 1572864 | tf_op jit(solution)/shard_map/all_to_all | solution.py:271
  39.7 15.4 %all-to-all-start.1 = ((bf16[8,192,128]{2,1,0:T(8,128)(2,1)}), bf16[8,192,128]{2,1,0:T(8,128)(2,1)S(1)}, u32[]{:S(2)}, u32[]{:S(2)}) async-start(bf16[8,192,128]{2,1,0:T(8,128)(2,1)} %get-tuple-element.17), calls=%async_computation.1 | async-start | bytes 786432 | tf_op jit(solution)/shard_map/all_to_all | solution.py:271
  43.2 20.5 %collective-permute-start.1 = (bf16[8,384,128]{2,1,0:T(8,128)(2,1)S(1)}, bf16[8,384,128]{2,1,0:T(8,128)(2,1)S(1)}, u32[]{:S(2)}, u32[]{:S(2)}) collective-permute-start(bf16[8,384,128]{2,1,0:T(8,128)(2,1)S(1)} %all-to-all-done), channel_id=1, source_target_pairs={{0,2},{1,3},{2,0},{3,1},{4,6},{5,7},{6,4},{7,5},{8,10},{9,11},{10,... | collective-permute-start | bytes 2359304 | tf_op jit(solution)/shard_map/ppermute | solution.py:274
  55.1 15.4 %all-to-all-start.2 = ((bf16[8,192,128]{2,1,0:T(8,128)(2,1)}), bf16[8,192,128]{2,1,0:T(8,128)(2,1)S(1)}, u32[]{:S(2)}, u32[]{:S(2)}) async-start(bf16[8,192,128]{2,1,0:T(8,128)(2,1)} %get-tuple-element.18), calls=%async_computation.2 | async-start | bytes 786432 | tf_op jit(solution)/shard_map/all_to_all | solution.py:271
  58.7 12.2 %collective-permute-start.3 = (bf16[8,192,128]{2,1,0:T(8,128)(2,1)S(1)}, bf16[8,192,128]{2,1,0:T(8,128)(2,1)}, u32[]{:S(2)}, u32[]{:S(2)}) collective-permute-start(bf16[8,192,128]{2,1,0:T(8,128)(2,1)S(1)} %all-to-all-done.1), channel_id=1, source_target_pairs={{0,2},{1,3},{2,0},{3,1},{4,6},{5,7},{6,4},{7,5},{8,10},{9,11},{10,... | collective-permute-start | bytes 1179656 | tf_op jit(solution)/shard_map/ppermute | solution.py:274
  60.3 12.2 %collective-permute-start = (bf16[8,384,128]{2,1,0:T(8,128)(2,1)S(1)}, bf16[8,384,128]{2,1,0:T(8,128)(2,1)S(1)}, u32[]{:S(2)}, u32[]{:S(2)}) collective-permute-start(bf16[8,384,128]{2,1,0:T(8,128)(2,1)S(1)} %all-to-all-done), channel_id=1, source_target_pairs={{0,1},{1,0},{2,3},{3,2},{4,5},{5,4},{6,7},{7,6},{8,9},{9,8},{10,11... | collective-permute-start | bytes 2359304 | tf_op jit(solution)/shard_map/ppermute | solution.py:277
  63.7 9.3 %collective-permute-start.2 = (bf16[8,384,128]{2,1,0:T(8,128)(2,1)S(1)}, bf16[8,384,128]{2,1,0:T(8,128)(2,1)}, u32[]{:S(2)}, u32[]{:S(2)}) collective-permute-start(bf16[8,384,128]{2,1,0:T(8,128)(2,1)S(1)} %collective-permute-done.1), channel_id=1, source_target_pairs={{0,1},{1,0},{2,3},{3,2},{4,5},{5,4},{6,7},{7,6},{8,9},{9,8},{10,11... | collective-permute-start | bytes 2359304 | tf_op jit(solution)/shard_map/ppermute | solution.py:277
  63.7 9.0 %collective-permute-start.6 = (bf16[8,192,128]{2,1,0:T(8,128)(2,1)S(1)}, bf16[8,192,128]{2,1,0:T(8,128)(2,1)}, u32[]{:S(2)}, u32[]{:S(2)}) collective-permute-start(bf16[8,192,128]{2,1,0:T(8,128)(2,1)S(1)} %all-to-all-done.1), channel_id=1, source_target_pairs={{0,1},{1,0},{2,3},{3,2},{4,5},{5,4},{6,7},{7,6},{8,9},{9,8},{10,11... | collective-permute-start | bytes 1179656 | tf_op jit(solution)/shard_map/ppermute | solution.py:277
  71.0 2.1 %collective-permute-start.7 = (bf16[8,192,128]{2,1,0:T(8,128)(2,1)}, bf16[8,192,128]{2,1,0:T(8,128)(2,1)}, u32[]{:S(2)}, u32[]{:S(2)}) collective-permute-start(bf16[8,192,128]{2,1,0:T(8,128)(2,1)} %collective-permute-done.3), channel_id=1, source_target_pairs={{0,1},{1,0},{2,3},{3,2},{4,5},{5,4},{6,7},{7,6},{8,9},{9,8},{10,11... | collective-permute-start | bytes 1179656 | tf_op jit(solution)/shard_map/ppermute | solution.py:277
  71.0 14.5 %collective-permute-start.5 = (bf16[8,192,128]{2,1,0:T(8,128)(2,1)S(1)}, bf16[8,192,128]{2,1,0:T(8,128)(2,1)S(1)}, u32[]{:S(2)}, u32[]{:S(2)}) collective-permute-start(bf16[8,192,128]{2,1,0:T(8,128)(2,1)S(1)} %all-to-all-done.2), channel_id=1, source_target_pairs={{0,2},{1,3},{2,0},{3,1},{4,6},{5,7},{6,4},{7,5},{8,10},{9,11},{10,... | collective-permute-start | bytes 1179656 | tf_op jit(solution)/shard_map/ppermute | solution.py:274
  72.5 13.1 %collective-permute-start.4 = (bf16[8,192,128]{2,1,0:T(8,128)(2,1)S(1)}, bf16[8,192,128]{2,1,0:T(8,128)(2,1)S(1)}, u32[]{:S(2)}, u32[]{:S(2)}) collective-permute-start(bf16[8,192,128]{2,1,0:T(8,128)(2,1)S(1)} %all-to-all-done.2), channel_id=1, source_target_pairs={{0,1},{1,0},{2,3},{3,2},{4,5},{5,4},{6,7},{7,6},{8,9},{9,8},{10,11... | collective-permute-start | bytes 1179656 | tf_op jit(solution)/shard_map/ppermute | solution.py:277
  85.5 1.7 %collective-permute-start.8 = (bf16[8,192,128]{2,1,0:T(8,128)(2,1)S(1)}, bf16[8,192,128]{2,1,0:T(8,128)(2,1)S(1)}, u32[]{:S(2)}, u32[]{:S(2)}) collective-permute-start(bf16[8,192,128]{2,1,0:T(8,128)(2,1)S(1)} %collective-permute-done.5), channel_id=1, source_target_pairs={{0,1},{1,0},{2,3},{3,2},{4,5},{5,4},{6,7},{7,6},{8,9},{9,8},{10,11... | collective-permute-start | bytes 1179656 | tf_op jit(solution)/shard_map/ppermute | solution.py:277
